TPU v7x, 32 devices: a whole 2x2x4 slice. The times are simulated.
32 devices in a mesh: section: 2 (over core), context: 8 (over z, x), tensor: 2 (over y).
Axes of the slice: x: 2, y: 2, z: 4, core: 2. Of those that a mesh axis runs over, the one named last changes fastest.
Arguments:
- boundary: bfloat16 [2, 2, 2048, 2048], P('section', None, ('context', 'tensor')), may hold values from -6 to 6
- token_places: int32 [2, 2048], P(None, 'context'), may hold values from 0 to 2047, as said below
- lengths: int32 [2, 3], replicated, may hold values from 1 to 1024, 2048 in all within a row
- qkv_weight: bfloat16 [2, 2048, 3, 2048], P('section', 'context', None, 'tensor'), may hold values from -0.125 to 0.125
- out_weight: bfloat16 [2, 2048, 2048], P('section', 'tensor', 'context'), may hold values from -1 to 1
- fc1_weight: bfloat16 [2, 2048, 8192], P('section', 'context', 'tensor'), may hold values from -0.125 to 0.125
- fc2_weight: bfloat16 [2, 8192, 2048], P('section', 'tensor', 'context'), may hold values from -0.0625 to 0.0625
- norm_gain: float32 [2, 2, 2048], P('section'), may hold values from 0.1 to 1.9
- norm_bias: float32 [2, 2, 2048], P('section'), may hold values from -4 to 4
- qkv_bias: float32 [2, 3, 2048], P('section'), may hold values from -4 to 4
- fc1_bias: float32 [2, 8192], P('section'), may hold values from -4 to 4
- branch_bias: float32 [2, 2, 2048], P('section'), may hold values from -4 to 4
Outputs:
- boundary_result: bfloat16 [2, 2, 2048, 2048], P('section', None, ('context', 'tensor'))
- qkv_weight_grad: float32 [2, 2048, 3, 2048], P('section', 'context', None, 'tensor')
- out_weight_grad: float32 [2, 2048, 2048], P('section', 'tensor', 'context')
- fc1_weight_grad: float32 [2, 2048, 8192], P('section', 'context', 'tensor')
- fc2_weight_grad: float32 [2, 8192, 2048], P('section', 'tensor', 'context')
- norm_gain_grad: float32 [2, 2, 2048], P('section')
- norm_bias_grad: float32 [2, 2, 2048], P('section')
- qkv_bias_grad: float32 [2, 3, 2048], P('section')
- fc1_bias_grad: float32 [2, 8192], P('section')
- branch_bias_grad: float32 [2, 2, 2048], P('section')
Inputs may be any that keep to these rules, and one draw needn't show every extreme that they name: `token_places`: in each micro-batch, the 256 entries of context index c are r_c, r_c + 8, r_c + 16 and so on, rising, for a permutation r of 0 to 7 drawn for each micro-batch; every packed position appears once. Each micro-batch's 3 lengths add up to 2048, and its longest is exactly 1024.
All inputs are finite; a program needn't handle non-finite values.
Results may differ from a plain program's by a relative error of at most 0.022.
Values may be sent and summed in bfloat16 or wider, within the bound.
No kernel may reach another device: no remote copies, remote signals or barrier semaphores. Data moves between devices by JAX's collectives and lax.ppermute only.
A program may use at most 384 MiB of HBM per device.

v0:
```python
import math

import jax
import jax.numpy as jnp
import numpy as np
from jax import lax
from jax.sharding import PartitionSpec as P

HD = 256
ROT = 64

EPSILON = 1e-05
ROTARY_BASE = 10000.0
MASKED = -1e30

BF16 = jnp.bfloat16
F32 = jnp.float32


def locate(placed, lengths):
    seq_ends = jnp.cumsum(lengths)
    seq_starts = seq_ends - lengths
    segment = jnp.sum((placed[:, None] >= seq_ends[None, :]).astype(jnp.int32), axis=1)
    chosen = segment[:, None] == jnp.arange(lengths.shape[0], dtype=jnp.int32)[None, :]
    seq_begin = jnp.sum(jnp.where(chosen, seq_starts[None, :], 0), axis=1)
    return (segment, placed - seq_begin)


def normalize_parts(values):
    row_mean = jnp.mean(values, axis=-1, keepdims=True)
    centered = values - row_mean
    inv_std = lax.rsqrt(jnp.mean(centered * centered, axis=-1, keepdims=True) + EPSILON)
    return (centered * inv_std, inv_std)


def angles(position):
    half_rot = ROT // 2
    frequency = ROTARY_BASE ** (-(jnp.arange(half_rot, dtype=F32) * 2.0) / ROT)
    phase_angle = position.astype(F32)[:, None] * frequency[None, :]
    return (jnp.cos(phase_angle), jnp.sin(phase_angle))


def rotate_pairs(values, cosine, sine_part):
    half_rot = ROT // 2
    leading = values[:, :half_rot]
    second = values[:, half_rot:ROT]
    return jnp.concatenate(
        [
            leading * cosine - second * sine_part,
            second * cosine + leading * sine_part,
            values[:, ROT:],
        ],
        axis=-1,
    )


def dot_tn(left_side, right_side):
    return lax.dot_general(
        left_side, right_side, (((0,), (0,)), ((), ())), preferred_element_type=F32
    )


def dot_nt(left_side, right_side):
    return lax.dot_general(
        left_side, right_side, (((1,), (1,)), ((), ())), preferred_element_type=F32
    )


def dot_nn(left_side, right_side):
    return jnp.dot(left_side, right_side, preferred_element_type=F32)


def pin(*values):
    return lax.optimization_barrier(values)


def flip(value, axis, mask):
    count = lax.axis_size(axis)
    return lax.ppermute(value, axis, [(place, place ^ mask) for place in range(count)])


def trade(value):
    return flip(value, "section", 1)


class Plan:
    def __init__(self, micro_count, heads_here, part_rows):
        self.contexts = lax.axis_size("context")
        self.tensors = lax.axis_size("tensor")
        self.heads = heads_here
        self.span = self.contexts // micro_count
        self.shares = self.span // heads_here
        self.part_rows = part_rows
        self.section = lax.axis_index("section")
        self.context = lax.axis_index("context")
        self.tensor = lax.axis_index("tensor")
        self.micro = self.context // self.span
        self.share = (self.context % self.span) // heads_here
        self.head = self.context % heads_here
        bits = [("context", 1 << b) for b in range(int(math.log2(heads_here)))]
        bits += [("tensor", 1 << b) for b in range(int(math.log2(self.tensors)))]
        ways = len(bits)
        cuts = [8 * ((part_rows // 8 * k + ways - 1) // ways) for k in range(ways + 1)]
        self.chunks = [(cuts[k], cuts[k + 1] - cuts[k]) for k in range(ways)]
        self.orders = [bits[k:] + bits[:k] for k in range(ways)]
        self.partners = 1 << ways
        head_flip, tensor_flip, row = [], [], []
        for (start, rows), order in zip(self.chunks, self.orders):
            for block in range(self.partners):
                masks = {"context": 0, "tensor": 0}
                for place, (axis, mask) in enumerate(order):
                    if block >> place & 1:
                        masks[axis] |= mask
                head_flip += [masks["context"]] * rows
                tensor_flip += [masks["tensor"]] * rows
                row += list(range(start, start + rows))
        self.head_flip = np.array(head_flip, np.int32)
        self.tensor_flip = np.array(tensor_flip, np.int32)
        self.row = np.array(row, np.int32)
        self.rows = len(row)

    def cut(self, full):
        return [
            full[start * self.partners : (start + rows) * self.partners]
            for start, rows in self.chunks
        ]

    def spread(self, *owns, pins=()):
        held = [own[start : start + rows] for own in owns for start, rows in self.chunks]
        orders = self.orders * len(owns)
        steps = len(self.chunks)
        for step in range(steps):
            came = [flip(v, *order[step]) for v, order in zip(held, orders)]
            came = list(pins[step](came) if step < len(pins) else pin(*came))
            if step < steps - 1:
                held = [jnp.concatenate([v, w], axis=0) for v, w in zip(held, came)]
                held = list(pin(*held))
        pairs = [v for pair in zip(held, came) for v in pair]
        each = len(pairs) // len(owns)
        return [jnp.concatenate(pairs[k : k + each], axis=0) for k in range(0, len(pairs), each)]

    def collect(self, *sets, pins=()):
        held = [part for parts in sets for part in parts]
        orders = self.orders * len(sets)
        steps = len(self.chunks)
        for count, step in enumerate(reversed(range(steps))):
            came = [flip(v[v.shape[0] // 2 :], *order[step]) for v, order in zip(held, orders)]
            came = list(pins[count](came) if count < len(pins) else pin(*came))
            held = [v[: v.shape[0] // 2].astype(F32) + w.astype(F32) for v, w in zip(held, came)]
            if step:
                held = list(pin(*[v.astype(BF16) for v in held]))
        return [jnp.concatenate(held[k : k + steps], axis=0) for k in range(0, len(held), steps)]

    def heads_of(self, full):
        return [
            full[start * self.partners : start * self.partners + 2 * rows]
            for start, rows in self.chunks
        ]

    def own_of(self, pairs):
        return jnp.concatenate([v[: v.shape[0] // 2] for v in pairs], axis=0)

    def sum_and_spread(self, parts, mix, sum_pins=(), spread_pins=()):
        steps = len(self.chunks)
        held = list(parts)
        for count, step in enumerate(range(steps - 1, 0, -1)):
            came = self.send_half(held, step)
            came = list(sum_pins[count](came) if count < len(sum_pins) else pin(*came))
            held = list(pin(*self.add_half(held, came)))
        came = self.send(held, 0)
        came = list(sum_pins[steps - 1](came) if len(sum_pins) >= steps else pin(*came))
        pairs = []
        for which, (v, w) in enumerate(zip(held, came)):
            half = v.shape[0] // 2
            swapped = jnp.concatenate([w[half:], w[:half]], axis=0)
            pairs.append(mix(which, v.astype(F32) + swapped.astype(F32)))
        pairs = list(pin(*pairs))
        held = pairs
        for count, step in enumerate(range(1, steps)):
            came = self.send(held, step)
            came = list(spread_pins[count](came) if count < len(spread_pins) else pin(*came))
            if step < steps - 1:
                held = list(pin(*self.join(held, came)))
        return self.own_of(pairs), self.whole(held, came)

    def pieces(self, own):
        return [own[start : start + rows] for start, rows in self.chunks]

    def send(self, held, step):
        return [flip(v, *order[step]) for v, order in zip(held, self.orders)]

    def join(self, held, came):
        return [jnp.concatenate([v, w], axis=0) for v, w in zip(held, came)]

    def whole(self, held, came):
        return jnp.concatenate([v for pair in zip(held, came) for v in pair], axis=0)

    def send_half(self, held, step):
        return [flip(v[v.shape[0] // 2 :], *order[step]) for v, order in zip(held, self.orders)]

    def add_half(self, held, came):
        return [
            (v[: v.shape[0] // 2].astype(F32) + w.astype(F32)).astype(BF16)
            for v, w in zip(held, came)
        ]

    def rows_of(self, places, section, share):
        context = section * self.span + share * self.heads + (self.head ^ self.head_flip)
        chosen = context[:, None] == jnp.arange(self.contexts, dtype=jnp.int32)[None, :]
        first = jnp.sum(jnp.where(chosen, places[None, :], 0), axis=1)
        within = (self.tensor ^ self.tensor_flip) * self.part_rows + self.row
        return first + within * self.contexts


def per_device(
    boundary,
    token_places,
    lengths,
    qkv_weight,
    out_weight,
    fc1_weight,
    fc2_weight,
    norm_gain,
    norm_bias,
    qkv_bias,
    fc1_bias,
    branch_bias,
):
    micro_count, part_rows, width = boundary.shape[1:]
    depth = qkv_weight.shape[1]
    heads_here = qkv_weight.shape[3] // HD
    units = fc1_weight.shape[2] // heads_here
    all_units = fc1_bias.shape[1]
    plan = Plan(micro_count, heads_here, part_rows)
    section, span, contexts = plan.section, plan.span, plan.contexts
    half_head, half_units = HD // 2, units // 2
    half_push = half_head + half_units
    copies = micro_count * plan.shares
    score_scale = 1.0 / math.sqrt(HD)
    head_index = plan.tensor * heads_here + plan.head

    def in_order(own, other):
        return (jnp.where(section == 0, own, other), jnp.where(section == 0, other, own))

    def flat(place_section, place_context):
        return place_section * contexts + place_context

    def bring(origin, held):
        came = []
        for micro in range(micro_count):
            pairs = [
                (flat(origin, side * span + k), flat(side, micro * span + k))
                for side in range(micro_count)
                for k in range(span)
            ]
            came.append(lax.ppermute(held[micro], ("section", "context"), pairs))
        return jnp.where(plan.micro == 0, came[0], came[1])

    def take_home(own, target):
        came = []
        for micro in range(micro_count):
            pairs = [
                (flat(side, micro * span + k), flat(target, side * span + k))
                for side in range(micro_count)
                for k in range(span)
            ]
            came.append(lax.ppermute(own, ("section", "context"), pairs))
        return jnp.stack(came)

    def half_of(halves):
        kept = lax.dynamic_index_in_dim(halves, section, 0, keepdims=False)
        return kept, trade(lax.dynamic_index_in_dim(halves, 1 - section, 0, keepdims=False))

    def exchange(blocks):
        return lax.all_to_all(blocks, "context", split_axis=0, concat_axis=0, tiled=True)

    def repeat(half, layer):
        blocks = in_order(*half)[layer]
        spread = jnp.broadcast_to(blocks[None], (copies,) + blocks.shape)
        return spread.reshape((contexts,) + blocks.shape[1:])

    def split_qkv():
        blocks = qkv_weight[0].reshape(depth, 3, heads_here, 2, half_head)
        return half_of(blocks.transpose(3, 2, 0, 1, 4).reshape(2, heads_here, depth, 3 * half_head))

    def split_fc1():
        blocks = fc1_weight[0].reshape(depth, heads_here, 2, half_units)
        return half_of(blocks.transpose(2, 1, 0, 3))

    def split_push():
        blocks = jnp.concatenate(
            [
                out_weight[0].reshape(heads_here, 2, half_head, depth),
                fc2_weight[0].reshape(heads_here, 2, half_units, depth),
            ],
            axis=2,
        )
        return half_of(blocks.transpose(1, 0, 2, 3))

    def join_qkv(dealt):
        own = dealt.reshape(width, 3, half_head)
        low, high = in_order(own, trade(own))
        return jnp.stack([low, high], axis=2).reshape(width, 3 * HD)

    def join_fc1(dealt):
        own = dealt.reshape(width, half_units)
        return jnp.concatenate([own, trade(own)], axis=1)

    def join_push(dealt):
        own = dealt.transpose(1, 0, 2).reshape(half_push, width)
        return jnp.concatenate([own, trade(own)], axis=0)

    def gather_places():
        first = lax.all_gather(token_places[:, 0], "context", axis=0)
        return lax.dynamic_index_in_dim(first, plan.micro, 1, keepdims=False)

    def find_places(places):
        own_lengths = lax.dynamic_index_in_dim(lengths, plan.micro, 0, keepdims=False)
        own_spot = locate(plan.rows_of(places, section, plan.share), own_lengths)
        key_spots = [
            locate(plan.rows_of(places, section ^ side, plan.share ^ share), own_lengths)
            for side in range(2)
            for share in range(plan.shares)
        ]
        return own_spot, [jnp.concatenate(part) for part in zip(*key_spots)]

    def share_keys(value):
        held = [value]
        for share in range(1, plan.shares):
            held.append(flip(value, "context", share * heads_here))
        pile = jnp.concatenate(held, axis=0)
        return jnp.concatenate([pile, trade(pile)], axis=0)

    def return_keys(value):
        half = value.shape[0] // 2
        pile = value[:half] + trade(value[half:].astype(BF16)).astype(F32)
        total = pile[: plan.rows]
        for share in range(1, plan.shares):
            piece = pile[share * plan.rows : (share + 1) * plan.rows].astype(BF16)
            total = total + flip(piece, "context", share * heads_here).astype(F32)
        return total

    own_vector = jnp.concatenate(
        [
            norm_gain[0].reshape(-1),
            norm_bias[0].reshape(-1),
            branch_bias[0, 0] + branch_bias[0, 1],
            lax.dynamic_slice(qkv_bias[0], (0, head_index * HD), (3, HD)).reshape(-1),
            lax.dynamic_slice_in_dim(fc1_bias[0], head_index * units, units),
        ]
    )

    def unit_order(values):
        first, second = in_order(values[..., :half_units], values[..., half_units:])
        return jnp.concatenate([first, second], axis=-1)

    def cut_vector(vector):
        gain = vector[: 2 * width].reshape(2, width)
        bias = vector[2 * width : 4 * width].reshape(2, width)
        out_shift = vector[4 * width : 5 * width]
        qkv_shift = vector[5 * width : 5 * width + 3 * HD]
        return gain, bias, out_shift, qkv_shift, unit_order(vector[5 * width + 3 * HD :])

    def scaled_rows(full_rows):
        return normalize_parts(full_rows.astype(F32))[0]

    def norms(full_rows, vectors):
        gain, bias = vectors[:2]
        scaled = scaled_rows(full_rows)
        return [(scaled * gain[k] + bias[k]).astype(BF16) for k in range(2)]

    def project(norm_attn, qkv_full, vectors):
        projected = dot_nn(norm_attn, qkv_full) + vectors[3]
        queries = rotate_pairs(projected[:, :HD], cosine, sine_part).astype(BF16)
        key_rows = rotate_pairs(projected[:, HD : 2 * HD], cosine, sine_part).astype(BF16)
        value_rows = projected[:, 2 * HD :].astype(BF16)
        key_value = share_keys(jnp.concatenate([key_rows, value_rows], axis=1))
        return queries, key_value[:, :HD], key_value[:, HD:]

    def attend(queries, keys, values):
        scores = dot_nt(queries, keys) * score_scale
        masked = jnp.where(allowed, scores, MASKED)
        top = jnp.max(masked, axis=1, keepdims=True)
        weight = jnp.where(allowed, jnp.exp(masked - top), 0.0)
        probs = weight / jnp.sum(weight, axis=1, keepdims=True)
        return dot_nn(probs.astype(BF16), values).astype(BF16), probs

    def score_grads(values, probs, d_attended):
        d_probs = dot_nt(d_attended, values)
        centre = jnp.sum(probs * d_probs, axis=1, keepdims=True)
        return (probs * (d_probs - centre)).astype(BF16)

    def attend_back(queries, keys, probs, d_scores, d_attended):
        d_queries = dot_nn(d_scores, keys) * score_scale
        d_keys = dot_tn(d_scores, queries) * score_scale
        d_values = dot_tn(probs.astype(BF16), d_attended)
        key_grads = return_keys(jnp.concatenate([d_keys, d_values], axis=1))
        return jnp.concatenate(
            [
                rotate_pairs(d_queries, cosine, -sine_part),
                rotate_pairs(key_grads[:, :HD], cosine, -sine_part),
                key_grads[:, HD:],
            ],
            axis=1,
        ).astype(BF16)

    def join_pushed(attended, hidden):
        first, second = in_order(attended[:, :half_head], attended[:, half_head:])
        return jnp.concatenate(
            [first, hidden[:, :half_units], second, hidden[:, half_units:]], axis=1
        )

    def cut_pushed(d_pushed):
        first, second = in_order(
            d_pushed[:, :half_head], d_pushed[:, half_push : half_push + half_head]
        )
        d_attended = jnp.concatenate([first, second], axis=1).astype(BF16)
        d_hidden = jnp.concatenate(
            [d_pushed[:, half_head:half_push], d_pushed[:, half_push + half_head :]], axis=1
        )
        return d_attended, d_hidden

    def push(pushed, push_full):
        return [dot_nn(rows, push_full).astype(BF16) for rows in plan.cut(pushed)]

    def add_branch(own_rows, summed, vectors):
        return (own_rows.astype(F32) + summed + vectors[2]).astype(BF16)

    def sum_cores(rows, own, other):
        came = trade(dot_tn(rows, other).astype(BF16))
        return (dot_tn(rows, own) + came.astype(F32)).astype(BF16)

    def push_blocks(pushed, grad_full):
        came = trade(dot_tn(pushed[:, half_push:], grad_full).astype(BF16))
        half = (dot_tn(pushed[:, :half_push], grad_full) + came.astype(F32)).astype(BF16)
        return half.reshape(half_push, contexts, depth).transpose(1, 0, 2)

    def fc1_blocks(norm_mlp, d_preact):
        half = sum_cores(norm_mlp, d_preact[:, :half_units], d_preact[:, half_units:])
        return half.reshape(contexts, depth, half_units)

    def qkv_blocks(norm_attn, d_projected):
        parts = d_projected.reshape(plan.rows, 3, 2, half_head)
        own, other = in_order(parts[:, :, 0], parts[:, :, 1])
        shape = (plan.rows, 3 * half_head)
        half = sum_cores(norm_attn, own.reshape(shape), other.reshape(shape))
        return half.reshape(contexts, depth, 3 * half_head)

    def gather_sum(came):
        return jnp.sum(came.reshape((copies, heads_here) + came.shape[1:]).astype(F32), axis=0)

    def norm_grads(d_projected, d_preact, qkv_full, fc1_full, full_rows, vectors, pin=None):
        d_norm_attn = dot_nt(d_projected, qkv_full)
        if pin is not None:
            d_norm_attn, d_preact = pin(d_norm_attn, d_preact)
        d_norm_mlp = dot_nt(d_preact, fc1_full)
        gain = vectors[0]
        d_scaled = (d_norm_attn * gain[0] + d_norm_mlp * gain[1]).astype(BF16)
        scaled = scaled_rows(full_rows)
        sums = [
            jnp.sum(d_norm_attn * scaled, axis=0),
            jnp.sum(d_norm_mlp * scaled, axis=0),
            jnp.sum(d_norm_attn, axis=0),
            jnp.sum(d_norm_mlp, axis=0),
        ]
        return d_scaled, sums

    def input_grad(grad_own, own_rows, d_scaled):
        own_scaled, own_inv = normalize_parts(own_rows.astype(F32))
        d_input = grad_own.astype(F32) + own_inv * (
            d_scaled
            - jnp.mean(d_scaled, axis=-1, keepdims=True)
            - own_scaled * jnp.mean(d_scaled * own_scaled, axis=-1, keepdims=True)
        )
        return d_input.astype(BF16)

    def vector_sums(norm_sums, d_projected, d_preact, grad_own):
        qkv_part = lax.dynamic_update_slice(
            jnp.zeros((3, width), F32),
            jnp.sum(d_projected, axis=0, dtype=F32).reshape(3, HD),
            (0, head_index * HD),
        )
        unit_part = lax.dynamic_update_slice_in_dim(
            jnp.zeros((all_units,), F32),
            unit_order(jnp.sum(d_preact, axis=0, dtype=F32)),
            head_index * units,
            0,
        )
        return jnp.concatenate(
            norm_sums
            + [jnp.sum(grad_own.astype(F32), axis=0), qkv_part.reshape(-1), unit_part]
        )

    def open_units(norm_mlp, fc1_full, vectors):
        preact = dot_nn(norm_mlp, fc1_full) + vectors[4]
        below = 0.5 * (1.0 + lax.erf(preact * math.sqrt(0.5)))
        bell = jnp.exp(-0.5 * preact * preact) * (1.0 / math.sqrt(2.0 * math.pi))
        return (preact * below).astype(BF16), below + preact * bell

    def finish(came0, came1):
        mine, yours = in_order(gather_sum(came0), gather_sum(came1))
        return jnp.stack(in_order(mine, trade(yours.astype(BF16)).astype(F32)))

    rows_in = [boundary[0, k] for k in range(micro_count)]
    first_rows = bring(0, rows_in)
    first_rows, qkv_weight, places, own_vector = pin(
        first_rows, qkv_weight, gather_places(), own_vector
    )
    qkv_half = split_qkv()

    def pin_gather(came):
        nonlocal qkv_half, own_vector, rows_in
        qkv_half, own_vector, rows_in, came = pin(qkv_half, own_vector, rows_in, came)
        return came

    full0 = plan.spread(first_rows, pins=[pin_gather])[0]
    qkv_in0 = repeat(qkv_half, 0)
    other_vector = trade(own_vector)
    grad1 = bring(1, rows_in)
    full0, qkv_in0, grad1, other_vector, fc1_weight, out_weight, fc2_weight = pin(
        full0, qkv_in0, grad1, other_vector, fc1_weight, out_weight, fc2_weight
    )
    (segment, position), (seg_keys, pos_keys) = find_places(places)
    fc1_half = split_fc1()
    fc1_in0 = repeat(fc1_half, 0)
    held1 = plan.pieces(grad1)
    vectors = [cut_vector(vector) for vector in in_order(own_vector, other_vector)]

    qkv_dealt0 = exchange(qkv_in0)
    norm_attn0, norm_mlp0 = norms(full0, vectors[0])
    push_half = split_push()
    qkv_dealt0, fc1_in0, push_half, norm_attn0, norm_mlp0, came1 = pin(
        qkv_dealt0, fc1_in0, push_half, norm_attn0, norm_mlp0, plan.send(held1, 0)
    )
    held1 = plan.join(held1, came1)
    fc1_dealt0 = exchange(fc1_in0)
    allowed = (segment[:, None] == seg_keys[None, :]) & (pos_keys[None, :] <= position[:, None])
    cosine, sine_part = angles(position)
    qkv0 = join_qkv(qkv_dealt0)
    queries0, keys0, values0 = project(norm_attn0, qkv0, vectors[0])
    push_in0 = repeat(push_half, 0)
    fc1_dealt0, push_in0, queries0, keys0, came1 = pin(
        fc1_dealt0, push_in0, queries0, keys0, plan.send(held1, 1)
    )
    held1 = plan.join(held1, came1)
    push_dealt0 = exchange(push_in0)
    attended0, probs0 = attend(queries0, keys0, values0)
    fc1_0 = join_fc1(fc1_dealt0)
    hidden0, slope0 = open_units(norm_mlp0, fc1_0, vectors[0])
    pushed0 = join_pushed(attended0, hidden0)
    qkv_in1, fc1_in1, push_in1 = [repeat(half, 1) for half in (qkv_half, fc1_half, push_half)]
    pushed0, probs0, slope0, push_dealt0, qkv_in1, fc1_in1, push_in1, came1 = pin(
        pushed0, probs0, slope0, push_dealt0, qkv_in1, fc1_in1, push_in1, plan.send(held1, 2)
    )
    grad_full1 = plan.whole(held1, came1)
    qkv_dealt1 = exchange(qkv_in1)
    push0 = join_push(push_dealt0)
    parts0 = push(pushed0, push0)

    def pin_deal(came):
        nonlocal qkv_dealt1
        qkv_dealt1, came = pin(qkv_dealt1, came)
        return came

    heads0 = plan.heads_of(full0)
    middle_rows, full1 = plan.sum_and_spread(
        parts0, lambda which, summed: add_branch(heads0[which], summed, vectors[0]), [pin_deal]
    )

    full1, qkv_dealt1, fc1_in1 = pin(full1, qkv_dealt1, fc1_in1)
    fc1_dealt1 = exchange(fc1_in1)
    qkv1 = join_qkv(qkv_dealt1)
    norm_attn1, norm_mlp1 = norms(full1, vectors[1])
    queries1, keys1, values1 = project(norm_attn1, qkv1, vectors[1])
    fc1_dealt1, push_in1, queries1, keys1 = pin(fc1_dealt1, push_in1, queries1, keys1)
    push_dealt1 = exchange(push_in1)
    attended1, probs1 = attend(queries1, keys1, values1)
    fc1_1 = join_fc1(fc1_dealt1)
    hidden1, slope1 = open_units(norm_mlp1, fc1_1, vectors[1])
    pushed1 = join_pushed(attended1, hidden1)
    push_back1 = push_blocks(pushed1, grad_full1)
    push_dealt1, push_back1, slope1, probs1 = pin(push_dealt1, push_back1, slope1, probs1)
    push_came1 = exchange(push_back1)
    push1 = join_push(push_dealt1)
    d_attended1, d_hidden1 = cut_pushed(dot_nt(grad_full1, push1))
    d_preact1 = (d_hidden1 * slope1).astype(BF16)
    fc1_back1 = fc1_blocks(norm_mlp1, d_preact1)
    d_scores1 = score_grads(values1, probs1, d_attended1)
    d_projected1 = attend_back(queries1, keys1, probs1, d_scores1, d_attended1)
    push_came1, fc1_back1, d_projected1 = pin(push_came1, fc1_back1, d_projected1)
    fc1_came1 = exchange(fc1_back1)
    d_scaled1, norm_sums1 = norm_grads(d_projected1, d_preact1, qkv1, fc1_1, full1, vectors[1])
    parts1 = plan.cut(d_scaled1)

    def pin_third(held):
        nonlocal fc1_came1
        fc1_came1, held = pin(fc1_came1, held)
        return held

    qkv_back1 = qkv_blocks(norm_attn1, d_projected1)
    last_parts = []

    def pin_push(came):
        nonlocal pushed1
        which = len(last_parts)
        part = dot_nn(plan.cut(pushed1)[which], push1).astype(BF16)
        part, pushed1, came = pin(part, pushed1, came)
        last_parts.append(part)
        return came

    grad_heads1, heads1 = plan.heads_of(grad_full1), plan.heads_of(full1)
    grad0, grad_full0 = plan.sum_and_spread(
        parts1,
        lambda which, summed: input_grad(grad_heads1[which], heads1[which], summed),
        [pin_third, pin_push, pin_push],
        [pin_push],
    )
    total1 = vector_sums(norm_sums1, d_projected1, d_preact1, grad1)

    grad_full0, qkv_back1, total1 = pin(grad_full0, qkv_back1, total1)
    qkv_came1 = exchange(qkv_back1)
    push_back0 = push_blocks(pushed0, grad_full0)
    push_back0, grad_full0, qkv_came1 = pin(push_back0, grad_full0, qkv_came1)
    push_came0 = exchange(push_back0)
    d_attended0, d_hidden0 = cut_pushed(dot_nt(grad_full0, push0))
    d_preact0 = (d_hidden0 * slope0).astype(BF16)
    fc1_back0 = fc1_blocks(norm_mlp0, d_preact0)
    d_scores0 = score_grads(values0, probs0, d_attended0)
    push_came0, fc1_back0, d_scores0, came = pin(
        push_came0, fc1_back0, d_scores0, plan.send_half(last_parts, 2)
    )
    last_parts = plan.add_half(last_parts, came)
    fc1_came0 = exchange(fc1_back0)
    d_projected0 = attend_back(queries0, keys0, probs0, d_scores0, d_attended0)
    qkv_back0 = qkv_blocks(norm_attn0, d_projected0)
    d_scaled0, norm_sums0 = norm_grads(d_projected0, d_preact0, qkv0, fc1_0, full0, vectors[0])
    fc1_came0, qkv_back0, d_scaled0, norm_sums0, push_came0, push_came1, came = pin(
        fc1_came0,
        qkv_back0,
        d_scaled0,
        norm_sums0,
        push_came0,
        push_came1,
        plan.send_half(last_parts, 1),
    )
    last_parts = plan.add_half(last_parts, came)
    total = jnp.stack([vector_sums(norm_sums0, d_projected0, d_preact0, grad0), total1])
    sums = [
        (axis, 1 << b)
        for axis in ("section", "context", "tensor")
        for b in range(int(math.log2(lax.axis_size(axis))))
    ]
    last_rows = last_home = None

    def pin_sum(came):
        nonlocal total, last_rows, last_home
        other = flip(total, *sums.pop(0))
        if last_rows is None:
            last_came, other, came = pin(plan.send_half(last_parts, 0), other, came)
            last_sum = [
                v[: v.shape[0] // 2].astype(F32) + w.astype(F32)
                for v, w in zip(last_parts, last_came)
            ]
            last_rows = add_branch(middle_rows, jnp.concatenate(last_sum, axis=0), vectors[1])
        elif last_home is None:
            last_home, other, came = pin(take_home(last_rows, 1), other, came)
        else:
            other, came = pin(other, came)
        total = total + other
        return came

    d_rows0 = plan.collect(plan.cut(d_scaled0), pins=[pin_sum] * len(plan.chunks))[0]
    d_input = input_grad(grad0, first_rows, d_rows0)
    qkv_back0, d_input, other, push_came0, push_came1, fc1_came0, fc1_came1 = pin(
        qkv_back0,
        d_input,
        flip(total, *sums.pop(0)),
        push_came0,
        push_came1,
        fc1_came0,
        fc1_came1,
    )
    total = total + other

    qkv_came0 = exchange(qkv_back0)
    first_home = take_home(d_input, 0)
    for spot in sums:
        total = total + flip(total, *spot)
    push_all = finish(push_came0, push_came1)
    fc1_all = finish(fc1_came0, fc1_came1)
    fc1_out = fc1_all.transpose(2, 1, 0, 3).reshape(depth, heads_here * units)
    out_out = push_all[:, :, :half_head].transpose(1, 0, 2, 3).reshape(heads_here * HD, depth)
    fc2_out = push_all[:, :, half_head:].transpose(1, 0, 2, 3).reshape(heads_here * units, depth)
    qkv_came0, last_home, fc1_out, out_out, fc2_out = pin(
        qkv_came0, last_home, fc1_out, out_out, fc2_out
    )
    result = jnp.where(section == 0, first_home, last_home)
    qkv_all = finish(qkv_came0, qkv_came1)
    qkv_out = (
        qkv_all.reshape(2, heads_here, depth, 3, half_head)
        .transpose(2, 3, 1, 0, 4)
        .reshape(depth, 3, heads_here * HD)
    )
    total = jnp.where(section == 0, total[0], total[1])
    return (
        result[None],
        qkv_out[None],
        out_out[None],
        fc1_out[None],
        fc2_out[None],
        total[: 2 * width].reshape(1, 2, width),
        total[2 * width : 4 * width].reshape(1, 2, width),
        total[5 * width : 8 * width].reshape(1, 3, width),
        total[8 * width :][None],
        jnp.broadcast_to(total[4 * width : 5 * width], (1, 2, width)),
    )


def solution(mesh):
    return jax.shard_map(
        per_device,
        mesh=mesh,
        in_specs=(
            P("section", None, ("context", "tensor"), None),
            P(None, "context"),
            P(),
            P("section", "context", None, "tensor"),
            P("section", "tensor", "context"),
            P("section", "context", "tensor"),
            P("section", "tensor", "context"),
            P("section", None, None),
            P("section", None, None),
            P("section", None, None),
            P("section", None),
            P("section", None, None),
        ),
        out_specs=(
            P("section", None, ("context", "tensor"), None),
            P("section", "context", None, "tensor"),
            P("section", "tensor", "context"),
            P("section", "context", "tensor"),
            P("section", "tensor", "context"),
            P("section", None, None),
            P("section", None, None),
            P("section", None, None),
            P("section", None),
            P("section", None, None),
        ),
        check_vma=False,
    )
```

profile of v0, /device:TPU:1, one launch (start us, length us, event | category | flops | bytes accessed | tf_op | source)
XLA Modules:
  0.0 986.4 jit_solution(16509631500462367376)
XLA Ops:
  7.0 10.4 %all-reduce.1 = s32[8,2]{1,0:T(8,128)S(1)} all-reduce(s32[8,2]{1,0:T(8,128)S(1)} %reshape.395), channel_id=2, replica_groups=mesh['section'=2,'context'=8,'tensor'=2] {'context'}, use_global_device_ids=true, to_apply=%add | all-reduce | flops 16 | bytes 128
  63.1 10.5 %collective-permute-done.10 = bf16[160,2048]{1,0:T(8,128)(2,1)S(1)} collective-permute-done((bf16[160,2048]{1,0:T(8,128)(2,1)}, bf16[160,2048]{1,0:T(8,128)(2,1)S(1)}, u32[]{:S(2)}, u32[]{:S(2)}) %collective-permute-start.10) | collective-permute-done | bytes 655392 | tf_op jit(solution)/shard_map/ppermute | solution.py:79
  106.7 6.3 fusion.22
  162.8 10.5 %collective-permute-done.24 = bf16[80,2048]{1,0:T(8,128)(2,1)} collective-permute-done((bf16[80,2048]{1,0:T(8,128)(2,1)S(1)}, bf16[80,2048]{1,0:T(8,128)(2,1)}, u32[]{:S(2)}, u32[]{:S(2)}) %collective-permute-start.24) | collective-permute-done | bytes 327712 | tf_op jit(solution)/shard_map/ppermute | solution.py:79
  173.3 5.3 collective-permute-done.22
  186.2 4.9 all-to-all-start.2
  213.4 9.8 fusion.35
  225.1 23.0 %collective-permute-done.28 = bf16[160,2048]{1,0:T(8,128)(2,1)} collective-permute-done((bf16[160,2048]{1,0:T(8,128)(2,1)S(1)}, bf16[160,2048]{1,0:T(8,128)(2,1)}, u32[]{:S(2)}, u32[]{:S(2)}) %collective-permute-start.28) | collective-permute-done | bytes 655392 | tf_op jit(solution)/shard_map/ppermute | solution.py:79
  261.0 5.3 convolution_convert_fusion.11
  273.8 5.6 convolution_convert_fusion.10
  281.4 15.2 %all-to-all-done.3 = bf16[8,256,384]{1,2,0:T(8,128)(2,1)S(1)} async-done(((bf16[8,256,384]{1,2,0:T(8,128)(2,1)}), bf16[8,256,384]{1,2,0:T(8,128)(2,1)S(1)}, u32[]{:S(2)}, u32[]{:S(2)}) %all-to-all-start.3) | async-done | bytes 1572896 | tf_op jit(solution)/shard_map/all_to_all | solution.py:275
  296.7 6.8 collective-permute-done.32
  310.6 5.9 collective-permute-done.35
  347.5 6.5 collective-permute-done.43
  368.2 5.2 collective-permute-start.45
  394.9 13.6 %all-to-all-done.4 = bf16[8,256,512]{2,1,0:T(8,128)(2,1)} async-done(((bf16[8,256,512]{2,1,0:T(8,128)(2,1)}), bf16[8,256,512]{2,1,0:T(8,128)(2,1)}, u32[]{:S(2)}, u32[]{:S(2)}) %all-to-all-start.4) | async-done | bytes 2097184 | tf_op jit(solution)/shard_map/all_to_all | solution.py:275
  408.4 7.7 all-to-all-start.5
  433.8 9.0 fusion.39
  449.1 4.9 collective-permute-done.48
  459.1 15.1 %all-to-all-done.5 = bf16[8,640,256]{1,2,0:T(8,128)(2,1)} async-done(((bf16[8,640,256]{1,2,0:T(8,128)(2,1)}), bf16[8,640,256]{1,2,0:T(8,128)(2,1)}, u32[]{:S(2)}, u32[]{:S(2)}) %all-to-all-start.5) | async-done | bytes 2621472 | tf_op jit(solution)/shard_map/all_to_all | solution.py:275
  490.1 9.0 fusion.226
  512.8 6.6 multiply_convert_fusion.1
  532.1 6.7 convolution_convert_fusion.4
  542.6 5.4 add_convert_fusion.5
  553.5 9.3 fusion.253
  562.9 10.4 %fusion.230 = (f32[2048]{0:T(1024)S(1)}, f32[2048]{0:T(1024)S(1)}, bf16[1024,2048]{1,0:T(8,128)(2,1)S(1)}, f32[2048]{0:T(1024)S(1)}, f32[2048]{0:T(1024)S(1)}) fusion(f32[1024]{0:T(1024)S(1)} %add_rsqrt_fusion, f32[1024]{0:T(1024)S(1)} %broadcast_multiply_fusion, bf16[1024,2048]{1,0:T(8,128)(2,1)S(1)} %copy-done.6, f32[2048]{0:T(1024)S(1)} %get-tuple-element.562, ...), kind=kOutput, calls=%fused_computation.550 | convolution fusion | flops 4330610688 | bytes 23126016 | tf_op jit(solution)/shard_map/dot_general | solution.py:64
  586.8 18.3 %collective-permute-done.54 = bf16[160,2048]{1,0:T(8,128)(2,1)} collective-permute-done((bf16[160,2048]{1,0:T(8,128)(2,1)}, bf16[160,2048]{1,0:T(8,128)(2,1)}, u32[]{:S(2)}, u32[]{:S(2)}) %collective-permute-start.54) | collective-permute-done | bytes 655392 | tf_op jit(solution)/shard_map/ppermute | solution.py:79
  613.6 7.7 collective-permute-done.57
  625.9 6.0 convolution_convert_fusion.9
  638.0 6.5 convolution_convert_fusion.8
  646.9 5.1 add_convert_fusion.7
  665.7 5.5 collective-permute-start.68
  683.2 5.7 add_convert_fusion.2
  690.6 21.2 %all-to-all-done.8 = bf16[8,256,384]{2,1,0:T(8,128)(2,1)S(1)} async-done(((bf16[8,256,384]{2,1,0:T(8,128)(2,1)}), bf16[8,256,384]{2,1,0:T(8,128)(2,1)S(1)}, u32[]{:S(2)}, u32[]{:S(2)}) %all-to-all-start.8) | async-done | bytes 1572896 | tf_op jit(solution)/shard_map/all_to_all | solution.py:275
  716.2 9.4 fusion.227
  741.8 8.6 multiply_convert_fusion
  750.4 7.0 add_convert_fusion.4
  757.4 17.3 %all-to-all-done.9 = bf16[8,640,256]{2,1,0:T(8,128)(2,1)} async-done(((bf16[8,640,256]{2,1,0:T(8,128)(2,1)}), bf16[8,640,256]{2,1,0:T(8,128)(2,1)}, u32[]{:S(2)}, u32[]{:S(2)}) %all-to-all-start.9) | async-done | bytes 2621472 | tf_op jit(solution)/shard_map/all_to_all | solution.py:275
  780.9 5.0 all-to-all-start.10
  814.1 5.8 fusion.254
  820.0 12.2 %fusion.228 = (f32[2048]{0:T(1024)S(1)}, f32[2048]{0:T(1024)}, bf16[1024,2048]{1,0:T(8,128)(2,1)}, f32[2048]{0:T(1024)}, f32[2048]{0:T(1024)}) fusion(f32[1024]{0:T(1024)S(1)} %copy-done.130, f32[1024]{0:T(1024)S(1)} %copy-done.123, bf16[1024,2048]{1,0:T(8,128)(2,1)S(1)} %copy-done.10, f32[2048]{0:T(1024)S(1)} %copy-done.126, f32[1024,2048]{1,0:T(8,128)} %fusion.254, ...), kind=kOutput, calls=%fused_computation.548 | convolution fusion | flops 4330610688 | bytes 23126016 | tf_op jit(solution)/shard_map/dot_general | solution.py:64
  850.0 13.2 %collective-permute-done.78 = bf16[48,2048]{1,0:T(8,128)(2,1)S(1)} collective-permute-done((bf16[48,2048]{1,0:T(8,128)(2,1)S(1)}, bf16[48,2048]{1,0:T(8,128)(2,1)S(1)}, u32[]{:S(2)}, u32[]{:S(2)}) %collective-permute-start.78) | collective-permute-done | bytes 196640 | tf_op jit(solution)/shard_map/ppermute | solution.py:79
  872.2 9.3 collective-permute-done.86
  900.1 10.5 %collective-permute-done.95 = f32[2,24576]{1,0:T(2,128)S(1)} collective-permute-done((f32[2,24576]{1,0:T(2,128)S(1)}, f32[2,24576]{1,0:T(2,128)S(1)}, u32[]{:S(2)}, u32[]{:S(2)}) %collective-permute-start.95) | collective-permute-done | bytes 196640 | tf_op jit(solution)/shard_map/ppermute | solution.py:79
  933.7 6.6 collective-permute-start.96
  943.7 5.3 copy.177
  949.0 5.5 fusion.55
  966.2 5.6 copy.186
  (892 shorter events, 555.4 us)
Async XLA Ops:
  2.0 18.6 %collective-permute-start.1 = (bf16[128,2048]{1,0:T(8,128)(2,1)S(1)}, bf16[128,2048]{1,0:T(8,128)(2,1)S(1)}, u32[]{:S(2)}, u32[]{:S(2)}) collective-permute-start(bf16[128,2048]{1,0:T(8,128)(2,1)S(1)} %get-tuple-element.222), channel_id=1, source_target_pairs={{0,8},{2,10},{4,12},{6,14},{8,24},{10,26},{12,28},{14,30},{1,9},{3... | collective-permute-start | bytes 1572872 | tf_op jit(solution)/shard_map/ppermute | solution.py:256
  2.7 18.8 %collective-permute-start = (bf16[128,2048]{1,0:T(8,128)(2,1)S(1)}, bf16[128,2048]{1,0:T(8,128)(2,1)S(1)}, u32[]{:S(2)}, u32[]{:S(2)}) collective-permute-start(bf16[128,2048]{1,0:T(8,128)(2,1)S(1)} %get-tuple-element.221), channel_id=1, source_target_pairs={{0,0},{2,2},{4,4},{6,6},{8,16},{10,18},{12,20},{14,22},{1,1},{3,3}... | collective-permute-start | bytes 1572872 | tf_op jit(solution)/shard_map/ppermute | solution.py:256
  38.7 21.9 %collective-permute-start.12 = (bf16[128,2048]{1,0:T(8,128)(2,1)}, bf16[128,2048]{1,0:T(8,128)(2,1)S(1)}, u32[]{:S(2)}, u32[]{:S(2)}) collective-permute-start(bf16[128,2048]{1,0:T(8,128)(2,1)} %copy-done.112), channel_id=1, source_target_pairs={{16,0},{18,2},{20,4},{22,6},{24,16},{26,18},{28,20},{30,22},{17,1}... | collective-permute-start | bytes 1572872 | tf_op jit(solution)/shard_map/ppermute | solution.py:256
  42.0 21.0 %collective-permute-start.13 = (bf16[128,2048]{1,0:T(8,128)(2,1)}, bf16[128,2048]{1,0:T(8,128)(2,1)}, u32[]{:S(2)}, u32[]{:S(2)}) collective-permute-start(bf16[128,2048]{1,0:T(8,128)(2,1)} %copy-done.111), channel_id=1, source_target_pairs={{16,8},{18,10},{20,12},{22,14},{24,24},{26,26},{28,28},{30,30},{17... | collective-permute-start | bytes 1572872 | tf_op jit(solution)/shard_map/ppermute | solution.py:256
  56.0 18.9 %collective-permute-start.9 = (bf16[192,2048]{1,0:T(8,128)(2,1)S(1)}, bf16[192,2048]{1,0:T(8,128)(2,1)}, u32[]{:S(2)}, u32[]{:S(2)}) collective-permute-start(bf16[192,2048]{1,0:T(8,128)(2,1)S(1)} %pad_maximum_fusion.21), channel_id=1, source_target_pairs={{0,1},{1,0},{2,3},{3,2},{4,5},{5,4},{6,7},{7,6},{8,9},{9,8},{10,11... | collective-permute-start | bytes 2359304 | tf_op jit(solution)/shard_map/ppermute | solution.py:79
  78.8 38.7 %all-to-all-start = ((bf16[8,256,384]{1,2,0:T(8,128)(2,1)}), bf16[8,256,384]{1,2,0:T(8,128)(2,1)}, u32[]{:S(2)}, u32[]{:S(2)}) async-start(bf16[8,256,384]{1,2,0:T(8,128)(2,1)} %bitcast.14), calls=%async_computation | async-start | bytes 3145728 | tf_op jit(solution)/shard_map/all_to_all | solution.py:275
  84.6 30.8 %collective-permute-start.19 = (bf16[40,2048]{1,0:T(8,128)(2,1)S(1)}, bf16[40,2048]{1,0:T(8,128)(2,1)S(1)}, u32[]{:S(2)}, u32[]{:S(2)}) collective-permute-start(bf16[40,2048]{1,0:T(8,128)(2,1)S(1)} %get-tuple-element.542), channel_id=1, source_target_pairs={{0,1},{1,0},{2,3},{3,2},{4,5},{5,4},{6,7},{7,6},{8,9},{9,8},{10,11... | collective-permute-start | bytes 491528 | tf_op jit(solution)/shard_map/ppermute | solution.py:79
  84.7 30.7 %collective-permute-start.18 = (bf16[40,2048]{1,0:T(8,128)(2,1)S(1)}, bf16[40,2048]{1,0:T(8,128)(2,1)S(1)}, u32[]{:S(2)}, u32[]{:S(2)}) collective-permute-start(bf16[40,2048]{1,0:T(8,128)(2,1)S(1)} %get-tuple-element.543), channel_id=1, source_target_pairs={{0,4},{2,6},{4,0},{6,2},{8,12},{10,14},{12,8},{14,10},{1,5},{3,7},... | collective-permute-start | bytes 491528 | tf_op jit(solution)/shard_map/ppermute | solution.py:79
  93.3 19.7 %collective-permute-start.15 = (bf16[4,256,512]{2,1,0:T(8,128)(2,1)}, bf16[4,256,512]{2,1,0:T(8,128)(2,1)}, u32[]{:S(2)}, u32[]{:S(2)}) collective-permute-start(bf16[4,256,512]{2,1,0:T(8,128)(2,1)} %bitcast.220), channel_id=1, source_target_pairs={{0,16},{16,0},{1,17},{17,1},{2,18},{18,2},{3,19},{19,3},{4,20},{20... | collective-permute-start | bytes 3145736 | tf_op jit(solution)/shard_map/ppermute | solution.py:79
  130.2 53.0 %all-to-all-start.1 = ((bf16[8,256,512]{2,1,0:T(8,128)(2,1)}), bf16[8,256,512]{2,1,0:T(8,128)(2,1)}, u32[]{:S(2)}, u32[]{:S(2)}) async-start(bf16[8,256,512]{2,1,0:T(8,128)(2,1)} %bitcast.20), calls=%async_computation.1 | async-start | bytes 4194304 | tf_op jit(solution)/shard_map/all_to_all | solution.py:275
  154.4 18.9 %collective-permute-start.24 = (bf16[80,2048]{1,0:T(8,128)(2,1)S(1)}, bf16[80,2048]{1,0:T(8,128)(2,1)}, u32[]{:S(2)}, u32[]{:S(2)}) collective-permute-start(bf16[80,2048]{1,0:T(8,128)(2,1)S(1)} %pad_maximum_fusion.48), channel_id=1, source_target_pairs={{0,2},{2,0},{4,6},{6,4},{8,10},{10,8},{12,14},{14,12},{1,3},{3,1},... | collective-permute-start | bytes 983048 | tf_op jit(solution)/shard_map/ppermute | solution.py:79
  156.3 22.3 %collective-permute-start.22 = (bf16[96,2048]{1,0:T(8,128)(2,1)S(1)}, bf16[96,2048]{1,0:T(8,128)(2,1)}, u32[]{:S(2)}, u32[]{:S(2)}) collective-permute-start(bf16[96,2048]{1,0:T(8,128)(2,1)S(1)} %pad_maximum_fusion.39), channel_id=1, source_target_pairs={{0,4},{2,6},{4,0},{6,2},{8,12},{10,14},{12,8},{14,10},{1,5},{3,7},... | collective-permute-start | bytes 1179656 | tf_op jit(solution)/shard_map/ppermute | solution.py:79
  186.2 63.7 %all-to-all-start.2 = ((bf16[8,640,256]{1,2,0:T(8,128)(2,1)}), bf16[8,640,256]{1,2,0:T(8,128)(2,1)}, u32[]{:S(2)}, u32[]{:S(2)}) async-start(bf16[8,640,256]{1,2,0:T(8,128)(2,1)} %bitcast.194), calls=%async_computation.2 | async-start | bytes 5242880 | tf_op jit(solution)/shard_map/all_to_all | solution.py:275
  193.4 54.8 %collective-permute-start.28 = (bf16[160,2048]{1,0:T(8,128)(2,1)S(1)}, bf16[160,2048]{1,0:T(8,128)(2,1)}, u32[]{:S(2)}, u32[]{:S(2)}) collective-permute-start(bf16[160,2048]{1,0:T(8,128)(2,1)S(1)} %pad_maximum_fusion.28), channel_id=1, source_target_pairs={{0,4},{2,6},{4,0},{6,2},{8,12},{10,14},{12,8},{14,10},{1,5},{3,7},... | collective-permute-start | bytes 1966088 | tf_op jit(solution)/shard_map/ppermute | solution.py:79
  194.8 53.3 %collective-permute-start.27 = (bf16[160,2048]{1,0:T(8,128)(2,1)S(1)}, bf16[160,2048]{1,0:T(8,128)(2,1)}, u32[]{:S(2)}, u32[]{:S(2)}) collective-permute-start(bf16[160,2048]{1,0:T(8,128)(2,1)S(1)} %pad_maximum_fusion.27), channel_id=1, source_target_pairs={{0,2},{2,0},{4,6},{6,4},{8,10},{10,8},{12,14},{14,12},{1,3},{3,1},... | collective-permute-start | bytes 1966088 | tf_op jit(solution)/shard_map/ppermute | solution.py:79
  197.1 51.1 %collective-permute-start.26 = (bf16[192,2048]{1,0:T(8,128)(2,1)S(1)}, bf16[192,2048]{1,0:T(8,128)(2,1)}, u32[]{:S(2)}, u32[]{:S(2)}) collective-permute-start(bf16[192,2048]{1,0:T(8,128)(2,1)S(1)} %pad_maximum_fusion.22), channel_id=1, source_target_pairs={{0,1},{1,0},{2,3},{3,2},{4,5},{5,4},{6,7},{7,6},{8,9},{9,8},{10,11... | collective-permute-start | bytes 2359304 | tf_op jit(solution)/shard_map/ppermute | solution.py:79
  256.1 40.6 %all-to-all-start.3 = ((bf16[8,256,384]{1,2,0:T(8,128)(2,1)}), bf16[8,256,384]{1,2,0:T(8,128)(2,1)S(1)}, u32[]{:S(2)}, u32[]{:S(2)}) async-start(bf16[8,256,384]{1,2,0:T(8,128)(2,1)} %bitcast.30), calls=%async_computation.3 | async-start | bytes 3145728 | tf_op jit(solution)/shard_map/all_to_all | solution.py:275
  267.6 29.1 %collective-permute-start.31 = (bf16[160,2048]{1,0:T(8,128)(2,1)}, bf16[160,2048]{1,0:T(8,128)(2,1)}, u32[]{:S(2)}, u32[]{:S(2)}) collective-permute-start(bf16[160,2048]{1,0:T(8,128)(2,1)} %slice.889), channel_id=1, source_target_pairs={{0,2},{2,0},{4,6},{6,4},{8,10},{10,8},{12,14},{14,12},{1,3},{3,1},... | collective-permute-start | bytes 1966088 | tf_op jit(solution)/shard_map/ppermute | solution.py:79
  273.7 29.8 %collective-permute-start.30 = (bf16[192,2048]{1,0:T(8,128)(2,1)S(1)}, bf16[192,2048]{1,0:T(8,128)(2,1)S(1)}, u32[]{:S(2)}, u32[]{:S(2)}) collective-permute-start(bf16[192,2048]{1,0:T(8,128)(2,1)S(1)} %slice.888), channel_id=1, source_target_pairs={{0,1},{1,0},{2,3},{3,2},{4,5},{5,4},{6,7},{7,6},{8,9},{9,8},{10,11... | collective-permute-start | bytes 2359304 | tf_op jit(solution)/shard_map/ppermute | solution.py:79
  280.4 23.2 %collective-permute-start.32 = (bf16[160,2048]{1,0:T(8,128)(2,1)}, bf16[160,2048]{1,0:T(8,128)(2,1)}, u32[]{:S(2)}, u32[]{:S(2)}) collective-permute-start(bf16[160,2048]{1,0:T(8,128)(2,1)} %slice.890), channel_id=1, source_target_pairs={{0,4},{2,6},{4,0},{6,2},{8,12},{10,14},{12,8},{14,10},{1,5},{3,7},... | collective-permute-start | bytes 1966088 | tf_op jit(solution)/shard_map/ppermute | solution.py:79
  359.0 49.4 %all-to-all-start.4 = ((bf16[8,256,512]{2,1,0:T(8,128)(2,1)}), bf16[8,256,512]{2,1,0:T(8,128)(2,1)}, u32[]{:S(2)}, u32[]{:S(2)}) async-start(bf16[8,256,512]{2,1,0:T(8,128)(2,1)} %bitcast.32), calls=%async_computation.4 | async-start | bytes 4194304 | tf_op jit(solution)/shard_map/all_to_all | solution.py:275
  408.4 65.7 %all-to-all-start.5 = ((bf16[8,640,256]{1,2,0:T(8,128)(2,1)}), bf16[8,640,256]{1,2,0:T(8,128)(2,1)}, u32[]{:S(2)}, u32[]{:S(2)}) async-start(bf16[8,640,256]{1,2,0:T(8,128)(2,1)} %bitcast.192), calls=%async_computation.5 | async-start | bytes 5242880 | tf_op jit(solution)/shard_map/all_to_all | solution.py:275
  485.7 64.1 %all-to-all-start.6 = ((bf16[8,640,256]{2,1,0:T(8,128)(2,1)}), bf16[8,640,256]{2,1,0:T(8,128)(2,1)}, u32[]{:S(2)}, u32[]{:S(2)}) async-start(bf16[8,640,256]{2,1,0:T(8,128)(2,1)} %bitcast.193), calls=%async_computation.6 | async-start | bytes 5242880 | tf_op jit(solution)/shard_map/all_to_all | solution.py:275
  508.0 34.5 %collective-permute-start.50 = (bf16[2048,512]{1,0:T(8,128)(2,1)}, bf16[2048,512]{1,0:T(8,128)(2,1)}, u32[]{:S(2)}, u32[]{:S(2)}) collective-permute-start(bf16[2048,512]{1,0:T(8,128)(2,1)} %convolution_convert_fusion.3), channel_id=1, source_target_pairs={{0,16},{16,0},{1,17},{17,1},{2,18},{18,2},{3,19},{19,3},{4,20},{20... | collective-permute-start | bytes 6291464 | tf_op jit(solution)/shard_map/ppermute | solution.py:79
  549.7 55.4 %all-to-all-start.7 = ((bf16[8,256,512]{2,1,0:T(8,128)(2,1)}), bf16[8,256,512]{2,1,0:T(8,128)(2,1)S(1)}, u32[]{:S(2)}, u32[]{:S(2)}) async-start(bf16[8,256,512]{2,1,0:T(8,128)(2,1)} %bitcast.216), calls=%async_computation.7 | async-start | bytes 4194304 | tf_op jit(solution)/shard_map/all_to_all | solution.py:275
  573.3 31.8 %collective-permute-start.52 = (bf16[192,2048]{1,0:T(8,128)(2,1)S(1)}, bf16[192,2048]{1,0:T(8,128)(2,1)}, u32[]{:S(2)}, u32[]{:S(2)}) collective-permute-start(bf16[192,2048]{1,0:T(8,128)(2,1)S(1)} %slice.928), channel_id=1, source_target_pairs={{0,1},{1,0},{2,3},{3,2},{4,5},{5,4},{6,7},{7,6},{8,9},{9,8},{10,11... | collective-permute-start | bytes 2359304 | tf_op jit(solution)/shard_map/ppermute | solution.py:79
  574.8 30.4 %collective-permute-start.54 = (bf16[160,2048]{1,0:T(8,128)(2,1)}, bf16[160,2048]{1,0:T(8,128)(2,1)}, u32[]{:S(2)}, u32[]{:S(2)}) collective-permute-start(bf16[160,2048]{1,0:T(8,128)(2,1)} %get-tuple-element.498), channel_id=1, source_target_pairs={{0,4},{2,6},{4,0},{6,2},{8,12},{10,14},{12,8},{14,10},{1,5},{3,7},... | collective-permute-start | bytes 1966088 | tf_op jit(solution)/shard_map/ppermute | solution.py:79
  576.2 28.9 %collective-permute-start.53 = (bf16[160,2048]{1,0:T(8,128)(2,1)}, bf16[160,2048]{1,0:T(8,128)(2,1)}, u32[]{:S(2)}, u32[]{:S(2)}) collective-permute-start(bf16[160,2048]{1,0:T(8,128)(2,1)} %get-tuple-element.499), channel_id=1, source_target_pairs={{0,2},{2,0},{4,6},{6,4},{8,10},{10,8},{12,14},{14,12},{1,3},{3,1},... | collective-permute-start | bytes 1966088 | tf_op jit(solution)/shard_map/ppermute | solution.py:79
  585.0 61.9 %collective-permute-start.67 = (bf16[2048,384]{1,0:T(8,128)(2,1)}, bf16[2048,384]{1,0:T(8,128)(2,1)}, u32[]{:S(2)}, u32[]{:S(2)}) collective-permute-start(bf16[2048,384]{1,0:T(8,128)(2,1)} %convolution_convert_fusion.7), channel_id=1, source_target_pairs={{0,16},{16,0},{1,17},{17,1},{2,18},{18,2},{3,19},{19,3},{4,20},{20... | collective-permute-start | bytes 4718600 | tf_op jit(solution)/shard_map/ppermute | solution.py:79
  671.2 40.5 %all-to-all-start.8 = ((bf16[8,256,384]{2,1,0:T(8,128)(2,1)}), bf16[8,256,384]{2,1,0:T(8,128)(2,1)S(1)}, u32[]{:S(2)}, u32[]{:S(2)}) async-start(bf16[8,256,384]{2,1,0:T(8,128)(2,1)} %bitcast.218), calls=%async_computation.8 | async-start | bytes 3145728 | tf_op jit(solution)/shard_map/all_to_all | solution.py:275
  678.0 79.4 %collective-permute-start.70 = (bf16[192,2048]{1,0:T(8,128)(2,1)}, bf16[192,2048]{1,0:T(8,128)(2,1)}, u32[]{:S(2)}, u32[]{:S(2)}) collective-permute-start(bf16[192,2048]{1,0:T(8,128)(2,1)} %slice.799), channel_id=1, source_target_pairs={{0,1},{1,0},{2,3},{3,2},{4,5},{5,4},{6,7},{7,6},{8,9},{9,8},{10,11... | collective-permute-start | bytes 2359304 | tf_op jit(solution)/shard_map/ppermute | solution.py:79
  679.6 77.8 %collective-permute-start.71 = (bf16[160,2048]{1,0:T(8,128)(2,1)S(1)}, bf16[160,2048]{1,0:T(8,128)(2,1)}, u32[]{:S(2)}, u32[]{:S(2)}) collective-permute-start(bf16[160,2048]{1,0:T(8,128)(2,1)S(1)} %slice.800), channel_id=1, source_target_pairs={{0,2},{2,0},{4,6},{6,4},{8,10},{10,8},{12,14},{14,12},{1,3},{3,1},... | collective-permute-start | bytes 1966088 | tf_op jit(solution)/shard_map/ppermute | solution.py:79
  682.0 75.4 %collective-permute-start.72 = (bf16[160,2048]{1,0:T(8,128)(2,1)}, bf16[160,2048]{1,0:T(8,128)(2,1)}, u32[]{:S(2)}, u32[]{:S(2)}) collective-permute-start(bf16[160,2048]{1,0:T(8,128)(2,1)} %slice.801), channel_id=1, source_target_pairs={{0,4},{2,6},{4,0},{6,2},{8,12},{10,14},{12,8},{14,10},{1,5},{3,7},... | collective-permute-start | bytes 1966088 | tf_op jit(solution)/shard_map/ppermute | solution.py:79
  711.8 62.9 %all-to-all-start.9 = ((bf16[8,640,256]{2,1,0:T(8,128)(2,1)}), bf16[8,640,256]{2,1,0:T(8,128)(2,1)}, u32[]{:S(2)}, u32[]{:S(2)}) async-start(bf16[8,640,256]{2,1,0:T(8,128)(2,1)} %bitcast.179), calls=%async_computation.9 | async-start | bytes 5242880 | tf_op jit(solution)/shard_map/all_to_all | solution.py:275
  780.9 55.0 %all-to-all-start.10 = ((bf16[8,256,512]{2,1,0:T(8,128)(2,1)}), bf16[8,256,512]{2,1,0:T(8,128)(2,1)}, u32[]{:S(2)}, u32[]{:S(2)}) async-start(bf16[8,256,512]{2,1,0:T(8,128)(2,1)} %bitcast.215), calls=%async_computation.10 | async-start | bytes 4194304 | tf_op jit(solution)/shard_map/all_to_all | solution.py:275
  789.3 46.5 %collective-permute-start.77 = (bf16[80,2048]{1,0:T(8,128)(2,1)}, bf16[80,2048]{1,0:T(8,128)(2,1)}, u32[]{:S(2)}, u32[]{:S(2)}) collective-permute-start(bf16[80,2048]{1,0:T(8,128)(2,1)} %slice.954), channel_id=1, source_target_pairs={{0,2},{2,0},{4,6},{6,4},{8,10},{10,8},{12,14},{14,12},{1,3},{3,1},... | collective-permute-start | bytes 983048 | tf_op jit(solution)/shard_map/ppermute | solution.py:79
  790.8 45.1 %collective-permute-start.76 = (bf16[80,2048]{1,0:T(8,128)(2,1)}, bf16[80,2048]{1,0:T(8,128)(2,1)}, u32[]{:S(2)}, u32[]{:S(2)}) collective-permute-start(bf16[80,2048]{1,0:T(8,128)(2,1)} %slice.953), channel_id=1, source_target_pairs={{0,1},{1,0},{2,3},{3,2},{4,5},{5,4},{6,7},{7,6},{8,9},{9,8},{10,11... | collective-permute-start | bytes 983048 | tf_op jit(solution)/shard_map/ppermute | solution.py:79
  791.8 44.1 %collective-permute-start.75 = (bf16[96,2048]{1,0:T(8,128)(2,1)}, bf16[96,2048]{1,0:T(8,128)(2,1)}, u32[]{:S(2)}, u32[]{:S(2)}) collective-permute-start(bf16[96,2048]{1,0:T(8,128)(2,1)} %slice.952), channel_id=1, source_target_pairs={{0,4},{2,6},{4,0},{6,2},{8,12},{10,14},{12,8},{14,10},{1,5},{3,7},... | collective-permute-start | bytes 1179656 | tf_op jit(solution)/shard_map/ppermute | solution.py:79
  811.9 20.3 %collective-permute-start.74 = (bf16[2048,384]{1,0:T(8,128)(2,1)S(1)}, bf16[2048,384]{1,0:T(8,128)(2,1)S(1)}, u32[]{:S(2)}, u32[]{:S(2)}) collective-permute-start(bf16[2048,384]{1,0:T(8,128)(2,1)S(1)} %convolution_convert_fusion.6), channel_id=1, source_target_pairs={{0,16},{16,0},{1,17},{17,1},{2,18},{18,2},{3,19},{19,3},{4,20},{20... | collective-permute-start | bytes 4718600 | tf_op jit(solution)/shard_map/ppermute | solution.py:79
  842.6 21.1 %collective-permute-start.82 = (bf16[192,2048]{1,0:T(8,128)(2,1)S(1)}, bf16[192,2048]{1,0:T(8,128)(2,1)S(1)}, u32[]{:S(2)}, u32[]{:S(2)}) collective-permute-start(bf16[192,2048]{1,0:T(8,128)(2,1)S(1)} %slice.830), channel_id=1, source_target_pairs={{0,1},{1,0},{2,3},{3,2},{4,5},{5,4},{6,7},{7,6},{8,9},{9,8},{10,11... | collective-permute-start | bytes 2359304 | tf_op jit(solution)/shard_map/ppermute | solution.py:79
  842.8 20.5 %collective-permute-start.84 = (bf16[160,2048]{1,0:T(8,128)(2,1)S(1)}, bf16[160,2048]{1,0:T(8,128)(2,1)S(1)}, u32[]{:S(2)}, u32[]{:S(2)}) collective-permute-start(bf16[160,2048]{1,0:T(8,128)(2,1)S(1)} %get-tuple-element.493), channel_id=1, source_target_pairs={{0,4},{2,6},{4,0},{6,2},{8,12},{10,14},{12,8},{14,10},{1,5},{3,7},... | collective-permute-start | bytes 1966088 | tf_op jit(solution)/shard_map/ppermute | solution.py:79
  844.0 19.3 %collective-permute-start.83 = (bf16[160,2048]{1,0:T(8,128)(2,1)S(1)}, bf16[160,2048]{1,0:T(8,128)(2,1)S(1)}, u32[]{:S(2)}, u32[]{:S(2)}) collective-permute-start(bf16[160,2048]{1,0:T(8,128)(2,1)S(1)} %get-tuple-element.494), channel_id=1, source_target_pairs={{0,2},{2,0},{4,6},{6,4},{8,10},{10,8},{12,14},{14,12},{1,3},{3,1},... | collective-permute-start | bytes 1966088 | tf_op jit(solution)/shard_map/ppermute | solution.py:79
  864.0 17.5 %collective-permute-start.86 = (bf16[128,2048]{1,0:T(8,128)(2,1)S(1)}, bf16[128,2048]{1,0:T(8,128)(2,1)S(1)}, u32[]{:S(2)}, u32[]{:S(2)}) collective-permute-start(bf16[128,2048]{1,0:T(8,128)(2,1)S(1)} %fusion.96), channel_id=1, source_target_pairs={{8,16},{10,18},{12,20},{14,22},{24,24},{26,26},{28,28},{30,30},{9,... | collective-permute-start | bytes 1572872 | tf_op jit(solution)/shard_map/ppermute | solution.py:267
  912.8 46.8 %all-to-all-start.11 = ((bf16[8,256,384]{2,1,0:T(8,128)(2,1)}), bf16[8,256,384]{2,1,0:T(8,128)(2,1)}, u32[]{:S(2)}, u32[]{:S(2)}) async-start(bf16[8,256,384]{2,1,0:T(8,128)(2,1)} %bitcast.217), calls=%async_computation.11 | async-start | bytes 3145728 | tf_op jit(solution)/shard_map/all_to_all | solution.py:275
  919.9 20.6 %collective-permute-start.98 = (bf16[4,256,512]{2,1,0:T(8,128)(2,1)S(1)}, bf16[4,256,512]{2,1,0:T(8,128)(2,1)S(1)}, u32[]{:S(2)}, u32[]{:S(2)}) collective-permute-start(bf16[4,256,512]{2,1,0:T(8,128)(2,1)S(1)} %select_convert_fusion.1), channel_id=1, source_target_pairs={{0,16},{16,0},{1,17},{17,1},{2,18},{18,2},{3,19},{19,3},{4,20},{20... | collective-permute-start | bytes 3145736 | tf_op jit(solution)/shard_map/ppermute | solution.py:79
  929.4 19.6 %collective-permute-start.99 = (bf16[4,640,256]{2,0,1:T(4,128)(2,1)}, bf16[4,640,256]{2,0,1:T(4,128)(2,1)}, u32[]{:S(2)}, u32[]{:S(2)}) collective-permute-start(bf16[4,640,256]{2,0,1:T(4,128)(2,1)} %select_convert_fusion), channel_id=1, source_target_pairs={{0,16},{16,0},{1,17},{17,1},{2,18},{18,2},{3,19},{19,3},{4,20},{20... | collective-permute-start | bytes 3932168 | tf_op jit(solution)/shard_map/ppermute | solution.py:79
  932.2 39.6 %collective-permute-start.97 = (bf16[128,2048]{1,0:T(8,128)(2,1)}, bf16[128,2048]{1,0:T(8,128)(2,1)}, u32[]{:S(2)}, u32[]{:S(2)}) collective-permute-start(bf16[128,2048]{1,0:T(8,128)(2,1)} %fusion.87), channel_id=1, source_target_pairs={{8,0},{10,2},{12,4},{14,6},{24,8},{26,10},{28,12},{30,14},{9,1},{1... | collective-permute-start | bytes 1572872 | tf_op jit(solution)/shard_map/ppermute | solution.py:267
  933.7 38.1 %collective-permute-start.96 = (bf16[128,2048]{1,0:T(8,128)(2,1)}, bf16[128,2048]{1,0:T(8,128)(2,1)}, u32[]{:S(2)}, u32[]{:S(2)}) collective-permute-start(bf16[128,2048]{1,0:T(8,128)(2,1)} %fusion.87), channel_id=1, source_target_pairs={{0,0},{2,2},{4,4},{6,6},{16,8},{18,10},{20,12},{22,14},{1,1},{3,3}... | collective-permute-start | bytes 1572872 | tf_op jit(solution)/shard_map/ppermute | solution.py:267
  (221 other events, 2156.0 us)
where the time goes:
time: 996 us; the launch traced here: 986 us
  waiting for transfers between devices  274 us (28%)
  matrix products  203 us (20%)
  starting transfers between devices  176 us (18%)
  other arithmetic  167 us (17%)
  local copies, waits for them, and re-layouts  151 us (15%)
  blocking collectives  10.4 us (1%)
    ppermute x94, waiting for transfers between devices, flip(): lax.ppermute(value, axis, [(place, place ^ mask) for place in range(count)])  171 us
    ppermute x94, starting transfers between devices, flip(): lax.ppermute(value, axis, [(place, place ^ mask) for place in range(count)])  97.7 us
    all_to_all x12, waiting for transfers between devices, exchange(): lax.all_to_all(blocks, 'context', split_axis=0, concat_axis=0, tiled=True)  92.6 us
    dot_general x10, matrix products, dot_nt(): lax.dot_general(left_side, right_side, (((1,), (1,)), ((), ())), preferre...  71.6 us
    dot_general x14, matrix products, dot_nn(): return jnp.dot(left_side, right_side, preferred_element_type=F32)  65.9 us
    dot_general x16, matrix products, dot_tn(): lax.dot_general(left_side, right_side, (((0,), (0,)), ((), ())), preferre...  65.2 us
    unnamed x362, local copies, waits for them, and re-layouts  61.7 us
    all_to_all x12, starting transfers between devices, exchange(): lax.all_to_all(blocks, 'context', split_axis=0, concat_axis=0, tiled=True)  55.6 us
  transfers between devices with their start and end apart: 114, of which 49 were waited for; matrix products, arithmetic and copies ran while one was open for 44% of the time, Pallas kernels for 0%

commit v1 on v0

--- a/solution.py
+++ b/solution.py
@@ -390,11 +390,14 @@
         centre = jnp.sum(probs * d_probs, axis=1, keepdims=True)
         return (probs * (d_probs - centre)).astype(BF16)
 
-    def attend_back(queries, keys, probs, d_scores, d_attended):
+    def head_grads(queries, keys, probs, d_scores, d_attended):
         d_queries = dot_nn(d_scores, keys) * score_scale
         d_keys = dot_tn(d_scores, queries) * score_scale
         d_values = dot_tn(probs.astype(BF16), d_attended)
-        key_grads = return_keys(jnp.concatenate([d_keys, d_values], axis=1))
+        return d_queries, jnp.concatenate([d_keys, d_values], axis=1)
+
+    def turn_back(d_queries, d_key_values):
+        key_grads = return_keys(d_key_values)
         return jnp.concatenate(
             [
                 rotate_pairs(d_queries, cosine, -sine_part),
@@ -586,7 +589,7 @@
     d_preact1 = (d_hidden1 * slope1).astype(BF16)
     fc1_back1 = fc1_blocks(norm_mlp1, d_preact1)
     d_scores1 = score_grads(values1, probs1, d_attended1)
-    d_projected1 = attend_back(queries1, keys1, probs1, d_scores1, d_attended1)
+    d_projected1 = turn_back(*head_grads(queries1, keys1, probs1, d_scores1, d_attended1))
     push_came1, fc1_back1, d_projected1 = pin(push_came1, fc1_back1, d_projected1)
     fc1_came1 = exchange(fc1_back1)
     d_scaled1, norm_sums1 = norm_grads(d_projected1, d_preact1, qkv1, fc1_1, full1, vectors[1])
@@ -626,12 +629,14 @@
     d_preact0 = (d_hidden0 * slope0).astype(BF16)
     fc1_back0 = fc1_blocks(norm_mlp0, d_preact0)
     d_scores0 = score_grads(values0, probs0, d_attended0)
-    push_came0, fc1_back0, d_scores0, came = pin(
-        push_came0, fc1_back0, d_scores0, plan.send_half(last_parts, 2)
-    )
+    head_grads0 = head_grads(queries0, keys0, probs0, d_scores0, d_attended0)
+    push_came0, fc1_back0, head_grads0, came = pin(
+        push_came0, fc1_back0, head_grads0, plan.send_half(last_parts, 2)
+    )
+    fc1_came0 = exchange(fc1_back0)
+    d_projected0 = turn_back(*head_grads0)
+    d_projected0, last_parts, came = pin(d_projected0, last_parts, came)
     last_parts = plan.add_half(last_parts, came)
-    fc1_came0 = exchange(fc1_back0)
-    d_projected0 = attend_back(queries0, keys0, probs0, d_scores0, d_attended0)
     qkv_back0 = qkv_blocks(norm_attn0, d_projected0)
     d_scaled0, norm_sums0 = norm_grads(d_projected0, d_preact0, qkv0, fc1_0, full0, vectors[0])
     fc1_came0, qkv_back0, d_scaled0, norm_sums0, push_came0, push_came1, came = pin(

time: 996 us -> 989 us (level)
  waiting for transfers between devices: 274 us -> 260 us
    unnamed x362 -> x358, local copies, waits for them, and re-layouts: 61.7 us -> 66.5 us
  transfers between devices with their start and end apart: 114 -> 114, of which waited for: 49 -> 48; matrix products, arithmetic and copies ran while one was open for 44% -> 45% of each run, Pallas kernels for 0% -> 0%
where the time goes in v1:
time: 989 us; the launch traced here: 979 us
  waiting for transfers between devices  260 us (26%)
  matrix products  205 us (21%)
  starting transfers between devices  177 us (18%)
  other arithmetic  166 us (17%)
  local copies, waits for them, and re-layouts  157 us (16%)
  blocking collectives  10.4 us (1%)
    ppermute x94, waiting for transfers between devices, flip(): lax.ppermute(value, axis, [(place, place ^ mask) for place in range(count)])  164 us
    ppermute x94, starting transfers between devices, flip(): lax.ppermute(value, axis, [(place, place ^ mask) for place in range(count)])  101 us
    all_to_all x12, waiting for transfers between devices, exchange(): lax.all_to_all(blocks, 'context', split_axis=0, concat_axis=0, tiled=True)  85.1 us
    dot_general x10, matrix products, dot_nt(): lax.dot_general(left_side, right_side, (((1,), (1,)), ((), ())), preferre...  71.3 us
    dot_general x14, matrix products, dot_nn(): return jnp.dot(left_side, right_side, preferred_element_type=F32)  69.3 us
    unnamed x358, local copies, waits for them, and re-layouts  66.5 us
    dot_general x16, matrix products, dot_tn(): lax.dot_general(left_side, right_side, (((0,), (0,)), ((), ())), preferre...  64 us
    all_to_all x12, starting transfers between devices, exchange(): lax.all_to_all(blocks, 'context', split_axis=0, concat_axis=0, tiled=True)  55.2 us
  transfers between devices with their start and end apart: 114, of which 48 were waited for; matrix products, arithmetic and copies ran while one was open for 45% of the time, Pallas kernels for 0%

profile of v1, /device:TPU:1, one launch (start us, length us, event | category | flops | bytes accessed | tf_op | source)
XLA Modules:
  0.0 979.4 jit_solution(2135858356433422159)
XLA Ops:
  7.0 10.4 %all-reduce.1 = s32[8,2]{1,0:T(8,128)S(1)} all-reduce(s32[8,2]{1,0:T(8,128)S(1)} %reshape.396), channel_id=2, replica_groups=mesh['section'=2,'context'=8,'tensor'=2] {'context'}, use_global_device_ids=true, to_apply=%add | all-reduce | flops 16 | bytes 128
  63.1 10.5 %collective-permute-done.10 = bf16[160,2048]{1,0:T(8,128)(2,1)S(1)} collective-permute-done((bf16[160,2048]{1,0:T(8,128)(2,1)}, bf16[160,2048]{1,0:T(8,128)(2,1)S(1)}, u32[]{:S(2)}, u32[]{:S(2)}) %collective-permute-start.10) | collective-permute-done | bytes 655392 | tf_op jit(solution)/shard_map/ppermute | solution.py:79
  78.8 4.8 all-to-all-start
  107.1 6.3 fusion.22
  163.1 10.5 %collective-permute-done.24 = bf16[80,2048]{1,0:T(8,128)(2,1)} collective-permute-done((bf16[80,2048]{1,0:T(8,128)(2,1)S(1)}, bf16[80,2048]{1,0:T(8,128)(2,1)}, u32[]{:S(2)}, u32[]{:S(2)}) %collective-permute-start.24) | collective-permute-done | bytes 327712 | tf_op jit(solution)/shard_map/ppermute | solution.py:79
  173.6 5.3 collective-permute-done.22
  213.5 9.8 %fusion.35 = (f32[1024,1024]{0,1:T(8,128)}, bf16[1024,1024]{0,1:T(8,128)(2,1)S(1)}) fusion(f32[1024]{0:T(1024)S(1)} %copy-done.140, bf16[1024,2048]{1,0:T(8,128)(2,1)S(1)} %copy-done.39, bf16[2048,512]{1,0:T(8,128)(2,1)S(1)} %collective-permute-done.25, bf16[2048,512]{1,0:T(8,128)(2,1)} %bitcast.29), kind=kOutput, calls=%fused_computation.58 | convolution fusion | flops 4314890240 | bytes 14684160 | tf_op jit(solution)/shard_map/dot_general | solution.py:70
  225.2 23.0 %collective-permute-done.28 = bf16[160,2048]{1,0:T(8,128)(2,1)} collective-permute-done((bf16[160,2048]{1,0:T(8,128)(2,1)S(1)}, bf16[160,2048]{1,0:T(8,128)(2,1)}, u32[]{:S(2)}, u32[]{:S(2)}) %collective-permute-start.28) | collective-permute-done | bytes 655392 | tf_op jit(solution)/shard_map/ppermute | solution.py:79
  261.1 5.2 convolution_convert_fusion.11
  274.0 5.6 convolution_convert_fusion.10
  281.8 15.2 %all-to-all-done.3 = bf16[8,256,384]{1,2,0:T(8,128)(2,1)S(1)} async-done(((bf16[8,256,384]{1,2,0:T(8,128)(2,1)}), bf16[8,256,384]{1,2,0:T(8,128)(2,1)S(1)}, u32[]{:S(2)}, u32[]{:S(2)}) %all-to-all-start.3) | async-done | bytes 1572896 | tf_op jit(solution)/shard_map/all_to_all | solution.py:275
  297.0 6.9 collective-permute-done.32
  310.8 5.8 collective-permute-done.35
  347.3 6.4 collective-permute-done.43
  367.8 5.4 collective-permute-start.45
  394.6 13.3 %all-to-all-done.4 = bf16[8,256,512]{2,1,0:T(8,128)(2,1)} async-done(((bf16[8,256,512]{2,1,0:T(8,128)(2,1)}), bf16[8,256,512]{2,1,0:T(8,128)(2,1)}, u32[]{:S(2)}, u32[]{:S(2)}) %all-to-all-start.4) | async-done | bytes 2097184 | tf_op jit(solution)/shard_map/all_to_all | solution.py:275
  407.9 7.6 all-to-all-start.5
  433.2 9.0 fusion.39
  448.5 4.9 collective-permute-done.48
  458.6 14.9 %all-to-all-done.5 = bf16[8,640,256]{1,2,0:T(8,128)(2,1)} async-done(((bf16[8,640,256]{1,2,0:T(8,128)(2,1)}), bf16[8,640,256]{1,2,0:T(8,128)(2,1)}, u32[]{:S(2)}, u32[]{:S(2)}) %all-to-all-start.5) | async-done | bytes 2621472 | tf_op jit(solution)/shard_map/all_to_all | solution.py:275
  488.4 9.0 fusion.225
  511.1 6.6 multiply_convert_fusion.1
  530.5 6.7 convolution_convert_fusion.4
  540.9 5.4 add_convert_fusion.5
  551.9 9.3 fusion.252
  561.2 10.4 %fusion.229 = (f32[2048]{0:T(1024)S(1)}, f32[2048]{0:T(1024)S(1)}, bf16[1024,2048]{1,0:T(8,128)(2,1)S(1)}, f32[2048]{0:T(1024)S(1)}, f32[2048]{0:T(1024)S(1)}) fusion(f32[1024]{0:T(1024)S(1)} %add_rsqrt_fusion, f32[1024]{0:T(1024)S(1)} %broadcast_multiply_fusion, bf16[1024,2048]{1,0:T(8,128)(2,1)S(1)} %copy-done.6, f32[2048]{0:T(1024)S(1)} %get-tuple-element.578, ...), kind=kOutput, calls=%fused_computation.553 | convolution fusion | flops 4330610688 | bytes 23126016 | tf_op jit(solution)/shard_map/dot_general | solution.py:64
  585.4 18.1 %collective-permute-done.54 = bf16[160,2048]{1,0:T(8,128)(2,1)} collective-permute-done((bf16[160,2048]{1,0:T(8,128)(2,1)}, bf16[160,2048]{1,0:T(8,128)(2,1)}, u32[]{:S(2)}, u32[]{:S(2)}) %collective-permute-start.54) | collective-permute-done | bytes 655392 | tf_op jit(solution)/shard_map/ppermute | solution.py:79
  612.2 7.5 collective-permute-done.57
  624.4 6.0 convolution_convert_fusion.9
  636.3 6.5 convolution_convert_fusion.8
  645.5 5.1 add_convert_fusion.7
  664.0 5.6 collective-permute-start.68
  681.6 5.7 add_convert_fusion.2
  689.0 21.1 %all-to-all-done.8 = bf16[8,256,384]{2,1,0:T(8,128)(2,1)S(1)} async-done(((bf16[8,256,384]{2,1,0:T(8,128)(2,1)}), bf16[8,256,384]{2,1,0:T(8,128)(2,1)S(1)}, u32[]{:S(2)}, u32[]{:S(2)}) %all-to-all-start.8) | async-done | bytes 1572896 | tf_op jit(solution)/shard_map/all_to_all | solution.py:275
  715.1 9.4 fusion.226
  739.0 8.6 multiply_convert_fusion
  761.7 5.3 add_convert_fusion.4
  767.1 6.9 all-to-all-done.9
  806.4 5.8 fusion.253
  812.3 11.8 %fusion.227 = (f32[2048]{0:T(1024)S(1)}, f32[2048]{0:T(1024)S(1)}, bf16[1024,2048]{1,0:T(8,128)(2,1)}, f32[2048]{0:T(1024)S(1)}, f32[2048]{0:T(1024)S(1)}) fusion(f32[1024]{0:T(1024)S(1)} %copy-done.135, f32[1024]{0:T(1024)S(1)} %copy-done.128, bf16[1024,2048]{1,0:T(8,128)(2,1)S(1)} %copy-done.10, f32[2048]{0:T(1024)S(1)} %copy-done.131, ...), kind=kOutput, calls=%fused_computation.551 | convolution fusion | flops 4330610688 | bytes 23126016 | tf_op jit(solution)/shard_map/dot_general | solution.py:64
  824.1 5.1 add_convert_fusion.6
  846.2 11.7 %collective-permute-done.78 = bf16[48,2048]{1,0:T(8,128)(2,1)S(1)} collective-permute-done((bf16[48,2048]{1,0:T(8,128)(2,1)S(1)}, bf16[48,2048]{1,0:T(8,128)(2,1)S(1)}, u32[]{:S(2)}, u32[]{:S(2)}) %collective-permute-start.78) | collective-permute-done | bytes 196640 | tf_op jit(solution)/shard_map/ppermute | solution.py:79
  866.3 9.7 collective-permute-done.86
  893.1 10.1 %collective-permute-done.95 = f32[2,24576]{1,0:T(2,128)S(1)} collective-permute-done((f32[2,24576]{1,0:T(2,128)S(1)}, f32[2,24576]{1,0:T(2,128)S(1)}, u32[]{:S(2)}, u32[]{:S(2)}) %collective-permute-start.95) | collective-permute-done | bytes 196640 | tf_op jit(solution)/shard_map/ppermute | solution.py:79
  926.3 6.0 collective-permute-start.96
  935.7 5.4 copy.183
  941.2 5.5 fusion.55
  959.2 5.6 copy.192
  (890 shorter events, 563.9 us)
Async XLA Ops:
  2.0 18.6 %collective-permute-start.1 = (bf16[128,2048]{1,0:T(8,128)(2,1)S(1)}, bf16[128,2048]{1,0:T(8,128)(2,1)S(1)}, u32[]{:S(2)}, u32[]{:S(2)}) collective-permute-start(bf16[128,2048]{1,0:T(8,128)(2,1)S(1)} %get-tuple-element.230), channel_id=1, source_target_pairs={{0,8},{2,10},{4,12},{6,14},{8,24},{10,26},{12,28},{14,30},{1,9},{3... | collective-permute-start | bytes 1572872 | tf_op jit(solution)/shard_map/ppermute | solution.py:256
  2.7 18.8 %collective-permute-start = (bf16[128,2048]{1,0:T(8,128)(2,1)S(1)}, bf16[128,2048]{1,0:T(8,128)(2,1)S(1)}, u32[]{:S(2)}, u32[]{:S(2)}) collective-permute-start(bf16[128,2048]{1,0:T(8,128)(2,1)S(1)} %get-tuple-element.229), channel_id=1, source_target_pairs={{0,0},{2,2},{4,4},{6,6},{8,16},{10,18},{12,20},{14,22},{1,1},{3,3}... | collective-permute-start | bytes 1572872 | tf_op jit(solution)/shard_map/ppermute | solution.py:256
  38.7 21.9 %collective-permute-start.12 = (bf16[128,2048]{1,0:T(8,128)(2,1)}, bf16[128,2048]{1,0:T(8,128)(2,1)S(1)}, u32[]{:S(2)}, u32[]{:S(2)}) collective-permute-start(bf16[128,2048]{1,0:T(8,128)(2,1)} %copy-done.114), channel_id=1, source_target_pairs={{16,0},{18,2},{20,4},{22,6},{24,16},{26,18},{28,20},{30,22},{17,1}... | collective-permute-start | bytes 1572872 | tf_op jit(solution)/shard_map/ppermute | solution.py:256
  42.0 21.0 %collective-permute-start.13 = (bf16[128,2048]{1,0:T(8,128)(2,1)}, bf16[128,2048]{1,0:T(8,128)(2,1)}, u32[]{:S(2)}, u32[]{:S(2)}) collective-permute-start(bf16[128,2048]{1,0:T(8,128)(2,1)} %copy-done.113), channel_id=1, source_target_pairs={{16,8},{18,10},{20,12},{22,14},{24,24},{26,26},{28,28},{30,30},{17... | collective-permute-start | bytes 1572872 | tf_op jit(solution)/shard_map/ppermute | solution.py:256
  56.0 18.9 %collective-permute-start.9 = (bf16[192,2048]{1,0:T(8,128)(2,1)S(1)}, bf16[192,2048]{1,0:T(8,128)(2,1)}, u32[]{:S(2)}, u32[]{:S(2)}) collective-permute-start(bf16[192,2048]{1,0:T(8,128)(2,1)S(1)} %pad_maximum_fusion.21), channel_id=1, source_target_pairs={{0,1},{1,0},{2,3},{3,2},{4,5},{5,4},{6,7},{7,6},{8,9},{9,8},{10,11... | collective-permute-start | bytes 2359304 | tf_op jit(solution)/shard_map/ppermute | solution.py:79
  78.8 39.1 %all-to-all-start = ((bf16[8,256,384]{1,2,0:T(8,128)(2,1)}), bf16[8,256,384]{1,2,0:T(8,128)(2,1)}, u32[]{:S(2)}, u32[]{:S(2)}) async-start(bf16[8,256,384]{1,2,0:T(8,128)(2,1)} %bitcast.14), calls=%async_computation | async-start | bytes 3145728 | tf_op jit(solution)/shard_map/all_to_all | solution.py:275
  84.9 30.8 %collective-permute-start.19 = (bf16[40,2048]{1,0:T(8,128)(2,1)S(1)}, bf16[40,2048]{1,0:T(8,128)(2,1)S(1)}, u32[]{:S(2)}, u32[]{:S(2)}) collective-permute-start(bf16[40,2048]{1,0:T(8,128)(2,1)S(1)} %get-tuple-element.558), channel_id=1, source_target_pairs={{0,1},{1,0},{2,3},{3,2},{4,5},{5,4},{6,7},{7,6},{8,9},{9,8},{10,11... | collective-permute-start | bytes 491528 | tf_op jit(solution)/shard_map/ppermute | solution.py:79
  85.0 30.7 %collective-permute-start.18 = (bf16[40,2048]{1,0:T(8,128)(2,1)S(1)}, bf16[40,2048]{1,0:T(8,128)(2,1)S(1)}, u32[]{:S(2)}, u32[]{:S(2)}) collective-permute-start(bf16[40,2048]{1,0:T(8,128)(2,1)S(1)} %get-tuple-element.559), channel_id=1, source_target_pairs={{0,4},{2,6},{4,0},{6,2},{8,12},{10,14},{12,8},{14,10},{1,5},{3,7},... | collective-permute-start | bytes 491528 | tf_op jit(solution)/shard_map/ppermute | solution.py:79
  93.7 19.7 %collective-permute-start.15 = (bf16[4,256,512]{2,1,0:T(8,128)(2,1)}, bf16[4,256,512]{2,1,0:T(8,128)(2,1)}, u32[]{:S(2)}, u32[]{:S(2)}) collective-permute-start(bf16[4,256,512]{2,1,0:T(8,128)(2,1)} %bitcast.224), channel_id=1, source_target_pairs={{0,16},{16,0},{1,17},{17,1},{2,18},{18,2},{3,19},{19,3},{4,20},{20... | collective-permute-start | bytes 3145736 | tf_op jit(solution)/shard_map/ppermute | solution.py:79
  130.5 52.9 %all-to-all-start.1 = ((bf16[8,256,512]{2,1,0:T(8,128)(2,1)}), bf16[8,256,512]{2,1,0:T(8,128)(2,1)}, u32[]{:S(2)}, u32[]{:S(2)}) async-start(bf16[8,256,512]{2,1,0:T(8,128)(2,1)} %bitcast.20), calls=%async_computation.1 | async-start | bytes 4194304 | tf_op jit(solution)/shard_map/all_to_all | solution.py:275
  154.7 18.9 %collective-permute-start.24 = (bf16[80,2048]{1,0:T(8,128)(2,1)S(1)}, bf16[80,2048]{1,0:T(8,128)(2,1)}, u32[]{:S(2)}, u32[]{:S(2)}) collective-permute-start(bf16[80,2048]{1,0:T(8,128)(2,1)S(1)} %pad_maximum_fusion.48), channel_id=1, source_target_pairs={{0,2},{2,0},{4,6},{6,4},{8,10},{10,8},{12,14},{14,12},{1,3},{3,1},... | collective-permute-start | bytes 983048 | tf_op jit(solution)/shard_map/ppermute | solution.py:79
  156.6 22.3 %collective-permute-start.22 = (bf16[96,2048]{1,0:T(8,128)(2,1)S(1)}, bf16[96,2048]{1,0:T(8,128)(2,1)}, u32[]{:S(2)}, u32[]{:S(2)}) collective-permute-start(bf16[96,2048]{1,0:T(8,128)(2,1)S(1)} %pad_maximum_fusion.39), channel_id=1, source_target_pairs={{0,4},{2,6},{4,0},{6,2},{8,12},{10,14},{12,8},{14,10},{1,5},{3,7},... | collective-permute-start | bytes 1179656 | tf_op jit(solution)/shard_map/ppermute | solution.py:79
  186.5 63.5 %all-to-all-start.2 = ((bf16[8,640,256]{1,2,0:T(8,128)(2,1)}), bf16[8,640,256]{1,2,0:T(8,128)(2,1)}, u32[]{:S(2)}, u32[]{:S(2)}) async-start(bf16[8,640,256]{1,2,0:T(8,128)(2,1)} %bitcast.198), calls=%async_computation.2 | async-start | bytes 5242880 | tf_op jit(solution)/shard_map/all_to_all | solution.py:275
  193.5 54.8 %collective-permute-start.28 = (bf16[160,2048]{1,0:T(8,128)(2,1)S(1)}, bf16[160,2048]{1,0:T(8,128)(2,1)}, u32[]{:S(2)}, u32[]{:S(2)}) collective-permute-start(bf16[160,2048]{1,0:T(8,128)(2,1)S(1)} %pad_maximum_fusion.28), channel_id=1, source_target_pairs={{0,4},{2,6},{4,0},{6,2},{8,12},{10,14},{12,8},{14,10},{1,5},{3,7},... | collective-permute-start | bytes 1966088 | tf_op jit(solution)/shard_map/ppermute | solution.py:79
  194.9 53.3 %collective-permute-start.27 = (bf16[160,2048]{1,0:T(8,128)(2,1)S(1)}, bf16[160,2048]{1,0:T(8,128)(2,1)}, u32[]{:S(2)}, u32[]{:S(2)}) collective-permute-start(bf16[160,2048]{1,0:T(8,128)(2,1)S(1)} %pad_maximum_fusion.27), channel_id=1, source_target_pairs={{0,2},{2,0},{4,6},{6,4},{8,10},{10,8},{12,14},{14,12},{1,3},{3,1},... | collective-permute-start | bytes 1966088 | tf_op jit(solution)/shard_map/ppermute | solution.py:79
  197.2 51.1 %collective-permute-start.26 = (bf16[192,2048]{1,0:T(8,128)(2,1)S(1)}, bf16[192,2048]{1,0:T(8,128)(2,1)}, u32[]{:S(2)}, u32[]{:S(2)}) collective-permute-start(bf16[192,2048]{1,0:T(8,128)(2,1)S(1)} %pad_maximum_fusion.22), channel_id=1, source_target_pairs={{0,1},{1,0},{2,3},{3,2},{4,5},{5,4},{6,7},{7,6},{8,9},{9,8},{10,11... | collective-permute-start | bytes 2359304 | tf_op jit(solution)/shard_map/ppermute | solution.py:79
  256.2 40.8 %all-to-all-start.3 = ((bf16[8,256,384]{1,2,0:T(8,128)(2,1)}), bf16[8,256,384]{1,2,0:T(8,128)(2,1)S(1)}, u32[]{:S(2)}, u32[]{:S(2)}) async-start(bf16[8,256,384]{1,2,0:T(8,128)(2,1)} %bitcast.30), calls=%async_computation.3 | async-start | bytes 3145728 | tf_op jit(solution)/shard_map/all_to_all | solution.py:275
  267.7 29.3 %collective-permute-start.31 = (bf16[160,2048]{1,0:T(8,128)(2,1)}, bf16[160,2048]{1,0:T(8,128)(2,1)}, u32[]{:S(2)}, u32[]{:S(2)}) collective-permute-start(bf16[160,2048]{1,0:T(8,128)(2,1)} %slice.891), channel_id=1, source_target_pairs={{0,2},{2,0},{4,6},{6,4},{8,10},{10,8},{12,14},{14,12},{1,3},{3,1},... | collective-permute-start | bytes 1966088 | tf_op jit(solution)/shard_map/ppermute | solution.py:79
  273.9 30.0 %collective-permute-start.30 = (bf16[192,2048]{1,0:T(8,128)(2,1)S(1)}, bf16[192,2048]{1,0:T(8,128)(2,1)S(1)}, u32[]{:S(2)}, u32[]{:S(2)}) collective-permute-start(bf16[192,2048]{1,0:T(8,128)(2,1)S(1)} %slice.890), channel_id=1, source_target_pairs={{0,1},{1,0},{2,3},{3,2},{4,5},{5,4},{6,7},{7,6},{8,9},{9,8},{10,11... | collective-permute-start | bytes 2359304 | tf_op jit(solution)/shard_map/ppermute | solution.py:79
  280.6 23.3 %collective-permute-start.32 = (bf16[160,2048]{1,0:T(8,128)(2,1)}, bf16[160,2048]{1,0:T(8,128)(2,1)}, u32[]{:S(2)}, u32[]{:S(2)}) collective-permute-start(bf16[160,2048]{1,0:T(8,128)(2,1)} %slice.892), channel_id=1, source_target_pairs={{0,4},{2,6},{4,0},{6,2},{8,12},{10,14},{12,8},{14,10},{1,5},{3,7},... | collective-permute-start | bytes 1966088 | tf_op jit(solution)/shard_map/ppermute | solution.py:79
  358.6 49.3 %all-to-all-start.4 = ((bf16[8,256,512]{2,1,0:T(8,128)(2,1)}), bf16[8,256,512]{2,1,0:T(8,128)(2,1)}, u32[]{:S(2)}, u32[]{:S(2)}) async-start(bf16[8,256,512]{2,1,0:T(8,128)(2,1)} %bitcast.32), calls=%async_computation.4 | async-start | bytes 4194304 | tf_op jit(solution)/shard_map/all_to_all | solution.py:275
  407.9 65.5 %all-to-all-start.5 = ((bf16[8,640,256]{1,2,0:T(8,128)(2,1)}), bf16[8,640,256]{1,2,0:T(8,128)(2,1)}, u32[]{:S(2)}, u32[]{:S(2)}) async-start(bf16[8,640,256]{1,2,0:T(8,128)(2,1)} %bitcast.195), calls=%async_computation.5 | async-start | bytes 5242880 | tf_op jit(solution)/shard_map/all_to_all | solution.py:275
  484.0 64.1 %all-to-all-start.6 = ((bf16[8,640,256]{2,1,0:T(8,128)(2,1)}), bf16[8,640,256]{2,1,0:T(8,128)(2,1)}, u32[]{:S(2)}, u32[]{:S(2)}) async-start(bf16[8,640,256]{2,1,0:T(8,128)(2,1)} %bitcast.196), calls=%async_computation.6 | async-start | bytes 5242880 | tf_op jit(solution)/shard_map/all_to_all | solution.py:275
  506.4 34.5 %collective-permute-start.50 = (bf16[2048,512]{1,0:T(8,128)(2,1)}, bf16[2048,512]{1,0:T(8,128)(2,1)}, u32[]{:S(2)}, u32[]{:S(2)}) collective-permute-start(bf16[2048,512]{1,0:T(8,128)(2,1)} %convolution_convert_fusion.3), channel_id=1, source_target_pairs={{0,16},{16,0},{1,17},{17,1},{2,18},{18,2},{3,19},{19,3},{4,20},{20... | collective-permute-start | bytes 6291464 | tf_op jit(solution)/shard_map/ppermute | solution.py:79
  548.1 55.4 %all-to-all-start.7 = ((bf16[8,256,512]{2,1,0:T(8,128)(2,1)}), bf16[8,256,512]{2,1,0:T(8,128)(2,1)S(1)}, u32[]{:S(2)}, u32[]{:S(2)}) async-start(bf16[8,256,512]{2,1,0:T(8,128)(2,1)} %bitcast.220), calls=%async_computation.7 | async-start | bytes 4194304 | tf_op jit(solution)/shard_map/all_to_all | solution.py:275
  571.7 31.8 %collective-permute-start.52 = (bf16[192,2048]{1,0:T(8,128)(2,1)S(1)}, bf16[192,2048]{1,0:T(8,128)(2,1)}, u32[]{:S(2)}, u32[]{:S(2)}) collective-permute-start(bf16[192,2048]{1,0:T(8,128)(2,1)S(1)} %slice.930), channel_id=1, source_target_pairs={{0,1},{1,0},{2,3},{3,2},{4,5},{5,4},{6,7},{7,6},{8,9},{9,8},{10,11... | collective-permute-start | bytes 2359304 | tf_op jit(solution)/shard_map/ppermute | solution.py:79
  573.3 30.2 %collective-permute-start.54 = (bf16[160,2048]{1,0:T(8,128)(2,1)}, bf16[160,2048]{1,0:T(8,128)(2,1)}, u32[]{:S(2)}, u32[]{:S(2)}) collective-permute-start(bf16[160,2048]{1,0:T(8,128)(2,1)} %get-tuple-element.514), channel_id=1, source_target_pairs={{0,4},{2,6},{4,0},{6,2},{8,12},{10,14},{12,8},{14,10},{1,5},{3,7},... | collective-permute-start | bytes 1966088 | tf_op jit(solution)/shard_map/ppermute | solution.py:79
  574.8 28.7 %collective-permute-start.53 = (bf16[160,2048]{1,0:T(8,128)(2,1)}, bf16[160,2048]{1,0:T(8,128)(2,1)}, u32[]{:S(2)}, u32[]{:S(2)}) collective-permute-start(bf16[160,2048]{1,0:T(8,128)(2,1)} %get-tuple-element.515), channel_id=1, source_target_pairs={{0,2},{2,0},{4,6},{6,4},{8,10},{10,8},{12,14},{14,12},{1,3},{3,1},... | collective-permute-start | bytes 1966088 | tf_op jit(solution)/shard_map/ppermute | solution.py:79
  583.6 61.9 %collective-permute-start.67 = (bf16[2048,384]{1,0:T(8,128)(2,1)}, bf16[2048,384]{1,0:T(8,128)(2,1)}, u32[]{:S(2)}, u32[]{:S(2)}) collective-permute-start(bf16[2048,384]{1,0:T(8,128)(2,1)} %convolution_convert_fusion.7), channel_id=1, source_target_pairs={{0,16},{16,0},{1,17},{17,1},{2,18},{18,2},{3,19},{19,3},{4,20},{20... | collective-permute-start | bytes 4718600 | tf_op jit(solution)/shard_map/ppermute | solution.py:79
  669.5 40.5 %all-to-all-start.8 = ((bf16[8,256,384]{2,1,0:T(8,128)(2,1)}), bf16[8,256,384]{2,1,0:T(8,128)(2,1)S(1)}, u32[]{:S(2)}, u32[]{:S(2)}) async-start(bf16[8,256,384]{2,1,0:T(8,128)(2,1)} %bitcast.222), calls=%async_computation.8 | async-start | bytes 3145728 | tf_op jit(solution)/shard_map/all_to_all | solution.py:275
  675.5 91.5 %collective-permute-start.70 = (bf16[192,2048]{1,0:T(8,128)(2,1)}, bf16[192,2048]{1,0:T(8,128)(2,1)}, u32[]{:S(2)}, u32[]{:S(2)}) collective-permute-start(bf16[192,2048]{1,0:T(8,128)(2,1)} %slice.801), channel_id=1, source_target_pairs={{0,1},{1,0},{2,3},{3,2},{4,5},{5,4},{6,7},{7,6},{8,9},{9,8},{10,11... | collective-permute-start | bytes 2359304 | tf_op jit(solution)/shard_map/ppermute | solution.py:79
  678.1 89.0 %collective-permute-start.71 = (bf16[160,2048]{1,0:T(8,128)(2,1)}, bf16[160,2048]{1,0:T(8,128)(2,1)}, u32[]{:S(2)}, u32[]{:S(2)}) collective-permute-start(bf16[160,2048]{1,0:T(8,128)(2,1)} %slice.802), channel_id=1, source_target_pairs={{0,2},{2,0},{4,6},{6,4},{8,10},{10,8},{12,14},{14,12},{1,3},{3,1},... | collective-permute-start | bytes 1966088 | tf_op jit(solution)/shard_map/ppermute | solution.py:79
  680.4 86.6 %collective-permute-start.72 = (bf16[160,2048]{1,0:T(8,128)(2,1)}, bf16[160,2048]{1,0:T(8,128)(2,1)}, u32[]{:S(2)}, u32[]{:S(2)}) collective-permute-start(bf16[160,2048]{1,0:T(8,128)(2,1)} %slice.803), channel_id=1, source_target_pairs={{0,4},{2,6},{4,0},{6,2},{8,12},{10,14},{12,8},{14,10},{1,5},{3,7},... | collective-permute-start | bytes 1966088 | tf_op jit(solution)/shard_map/ppermute | solution.py:79
  711.2 62.7 %all-to-all-start.9 = ((bf16[8,640,256]{2,1,0:T(8,128)(2,1)}), bf16[8,640,256]{2,1,0:T(8,128)(2,1)S(1)}, u32[]{:S(2)}, u32[]{:S(2)}) async-start(bf16[8,640,256]{2,1,0:T(8,128)(2,1)} %bitcast.197), calls=%async_computation.9 | async-start | bytes 5242880 | tf_op jit(solution)/shard_map/all_to_all | solution.py:275
  733.4 26.4 %collective-permute-start.69 = (bf16[2048,512]{1,0:T(8,128)(2,1)}, bf16[2048,512]{1,0:T(8,128)(2,1)}, u32[]{:S(2)}, u32[]{:S(2)}) collective-permute-start(bf16[2048,512]{1,0:T(8,128)(2,1)} %convolution_convert_fusion.2), channel_id=1, source_target_pairs={{0,16},{16,0},{1,17},{17,1},{2,18},{18,2},{3,19},{19,3},{4,20},{20... | collective-permute-start | bytes 6291464 | tf_op jit(solution)/shard_map/ppermute | solution.py:79
  780.5 53.0 %all-to-all-start.10 = ((bf16[8,256,512]{2,1,0:T(8,128)(2,1)}), bf16[8,256,512]{2,1,0:T(8,128)(2,1)}, u32[]{:S(2)}, u32[]{:S(2)}) async-start(bf16[8,256,512]{2,1,0:T(8,128)(2,1)} %bitcast.219), calls=%async_computation.10 | async-start | bytes 4194304 | tf_op jit(solution)/shard_map/all_to_all | solution.py:275
  794.9 35.7 %collective-permute-start.75 = (bf16[96,2048]{1,0:T(8,128)(2,1)S(1)}, bf16[96,2048]{1,0:T(8,128)(2,1)}, u32[]{:S(2)}, u32[]{:S(2)}) collective-permute-start(bf16[96,2048]{1,0:T(8,128)(2,1)S(1)} %slice.951), channel_id=1, source_target_pairs={{0,4},{2,6},{4,0},{6,2},{8,12},{10,14},{12,8},{14,10},{1,5},{3,7},... | collective-permute-start | bytes 1179656 | tf_op jit(solution)/shard_map/ppermute | solution.py:79
  797.7 31.5 %collective-permute-start.76 = (bf16[80,2048]{1,0:T(8,128)(2,1)S(1)}, bf16[80,2048]{1,0:T(8,128)(2,1)S(1)}, u32[]{:S(2)}, u32[]{:S(2)}) collective-permute-start(bf16[80,2048]{1,0:T(8,128)(2,1)S(1)} %slice.952), channel_id=1, source_target_pairs={{0,1},{1,0},{2,3},{3,2},{4,5},{5,4},{6,7},{7,6},{8,9},{9,8},{10,11... | collective-permute-start | bytes 983048 | tf_op jit(solution)/shard_map/ppermute | solution.py:79
  800.1 29.1 %collective-permute-start.77 = (bf16[80,2048]{1,0:T(8,128)(2,1)S(1)}, bf16[80,2048]{1,0:T(8,128)(2,1)S(1)}, u32[]{:S(2)}, u32[]{:S(2)}) collective-permute-start(bf16[80,2048]{1,0:T(8,128)(2,1)S(1)} %slice.953), channel_id=1, source_target_pairs={{0,2},{2,0},{4,6},{6,4},{8,10},{10,8},{12,14},{14,12},{1,3},{3,1},... | collective-permute-start | bytes 983048 | tf_op jit(solution)/shard_map/ppermute | solution.py:79
  805.1 19.0 %collective-permute-start.74 = (bf16[2048,384]{1,0:T(8,128)(2,1)}, bf16[2048,384]{1,0:T(8,128)(2,1)}, u32[]{:S(2)}, u32[]{:S(2)}) collective-permute-start(bf16[2048,384]{1,0:T(8,128)(2,1)} %convolution_convert_fusion.6), channel_id=1, source_target_pairs={{0,16},{16,0},{1,17},{17,1},{2,18},{18,2},{3,19},{19,3},{4,20},{20... | collective-permute-start | bytes 4718600 | tf_op jit(solution)/shard_map/ppermute | solution.py:79
  836.9 21.4 %collective-permute-start.82 = (bf16[192,2048]{1,0:T(8,128)(2,1)S(1)}, bf16[192,2048]{1,0:T(8,128)(2,1)S(1)}, u32[]{:S(2)}, u32[]{:S(2)}) collective-permute-start(bf16[192,2048]{1,0:T(8,128)(2,1)S(1)} %slice.832), channel_id=1, source_target_pairs={{0,1},{1,0},{2,3},{3,2},{4,5},{5,4},{6,7},{7,6},{8,9},{9,8},{10,11... | collective-permute-start | bytes 2359304 | tf_op jit(solution)/shard_map/ppermute | solution.py:79
  838.0 20.0 %collective-permute-start.84 = (bf16[160,2048]{1,0:T(8,128)(2,1)S(1)}, bf16[160,2048]{1,0:T(8,128)(2,1)S(1)}, u32[]{:S(2)}, u32[]{:S(2)}) collective-permute-start(bf16[160,2048]{1,0:T(8,128)(2,1)S(1)} %get-tuple-element.509), channel_id=1, source_target_pairs={{0,4},{2,6},{4,0},{6,2},{8,12},{10,14},{12,8},{14,10},{1,5},{3,7},... | collective-permute-start | bytes 1966088 | tf_op jit(solution)/shard_map/ppermute | solution.py:79
  839.4 18.5 %collective-permute-start.83 = (bf16[160,2048]{1,0:T(8,128)(2,1)S(1)}, bf16[160,2048]{1,0:T(8,128)(2,1)S(1)}, u32[]{:S(2)}, u32[]{:S(2)}) collective-permute-start(bf16[160,2048]{1,0:T(8,128)(2,1)S(1)} %get-tuple-element.510), channel_id=1, source_target_pairs={{0,2},{2,0},{4,6},{6,4},{8,10},{10,8},{12,14},{14,12},{1,3},{3,1},... | collective-permute-start | bytes 1966088 | tf_op jit(solution)/shard_map/ppermute | solution.py:79
  905.4 46.9 %all-to-all-start.11 = ((bf16[8,256,384]{2,1,0:T(8,128)(2,1)}), bf16[8,256,384]{2,1,0:T(8,128)(2,1)}, u32[]{:S(2)}, u32[]{:S(2)}) async-start(bf16[8,256,384]{2,1,0:T(8,128)(2,1)} %bitcast.221), calls=%async_computation.11 | async-start | bytes 3145728 | tf_op jit(solution)/shard_map/all_to_all | solution.py:275
  912.9 19.6 %collective-permute-start.98 = (bf16[4,256,512]{2,1,0:T(8,128)(2,1)S(1)}, bf16[4,256,512]{2,1,0:T(8,128)(2,1)S(1)}, u32[]{:S(2)}, u32[]{:S(2)}) collective-permute-start(bf16[4,256,512]{2,1,0:T(8,128)(2,1)S(1)} %select_convert_fusion.1), channel_id=1, source_target_pairs={{0,16},{16,0},{1,17},{17,1},{2,18},{18,2},{3,19},{19,3},{4,20},{20... | collective-permute-start | bytes 3145736 | tf_op jit(solution)/shard_map/ppermute | solution.py:79
  921.1 20.0 %collective-permute-start.99 = (bf16[4,640,256]{2,0,1:T(4,128)(2,1)}, bf16[4,640,256]{2,0,1:T(4,128)(2,1)}, u32[]{:S(2)}, u32[]{:S(2)}) collective-permute-start(bf16[4,640,256]{2,0,1:T(4,128)(2,1)} %select_convert_fusion), channel_id=1, source_target_pairs={{0,16},{16,0},{1,17},{17,1},{2,18},{18,2},{3,19},{19,3},{4,20},{20... | collective-permute-start | bytes 3932168 | tf_op jit(solution)/shard_map/ppermute | solution.py:79
  924.9 39.9 %collective-permute-start.97 = (bf16[128,2048]{1,0:T(8,128)(2,1)}, bf16[128,2048]{1,0:T(8,128)(2,1)}, u32[]{:S(2)}, u32[]{:S(2)}) collective-permute-start(bf16[128,2048]{1,0:T(8,128)(2,1)} %fusion.84), channel_id=1, source_target_pairs={{8,0},{10,2},{12,4},{14,6},{24,8},{26,10},{28,12},{30,14},{9,1},{1... | collective-permute-start | bytes 1572872 | tf_op jit(solution)/shard_map/ppermute | solution.py:267
  926.3 38.5 %collective-permute-start.96 = (bf16[128,2048]{1,0:T(8,128)(2,1)}, bf16[128,2048]{1,0:T(8,128)(2,1)}, u32[]{:S(2)}, u32[]{:S(2)}) collective-permute-start(bf16[128,2048]{1,0:T(8,128)(2,1)} %fusion.84), channel_id=1, source_target_pairs={{0,0},{2,2},{4,4},{6,6},{16,8},{18,10},{20,12},{22,14},{1,1},{3,3}... | collective-permute-start | bytes 1572872 | tf_op jit(solution)/shard_map/ppermute | solution.py:267
  (219 other events, 2101.3 us)

commit v2 on v1

--- a/solution.py
+++ b/solution.py
@@ -696,9 +696,7 @@
     fc1_out = fc1_all.transpose(2, 1, 0, 3).reshape(depth, heads_here * units)
     out_out = push_all[:, :, :half_head].transpose(1, 0, 2, 3).reshape(heads_here * HD, depth)
     fc2_out = push_all[:, :, half_head:].transpose(1, 0, 2, 3).reshape(heads_here * units, depth)
-    qkv_came0, last_home, fc1_out, out_out, fc2_out = pin(
-        qkv_came0, last_home, fc1_out, out_out, fc2_out
-    )
+    qkv_came0, last_home = pin(qkv_came0, last_home)
     result = jnp.where(section == 0, first_home, last_home)
     qkv_all = finish(qkv_came0, qkv_came1)
     qkv_out = (

time: 989 us -> 984 us (level)
    unnamed x358 -> x362, local copies, waits for them, and re-layouts: 66.5 us -> 66.4 us
  transfers between devices with their start and end apart: 114 -> 114, of which waited for: 48 -> 46; matrix products, arithmetic and copies ran while one was open for 45% -> 46% of each run, Pallas kernels for 0% -> 0%
where the time goes in v2:
time: 984 us; the launch traced here: 975 us
  waiting for transfers between devices  257 us (26%)
  matrix products  205 us (21%)
  starting transfers between devices  176 us (18%)
  other arithmetic  166 us (17%)
  local copies, waits for them, and re-layouts  156 us (16%)
  blocking collectives  10.4 us (1%)
    ppermute x94, waiting for transfers between devices, flip(): lax.ppermute(value, axis, [(place, place ^ mask) for place in range(count)])  163 us
    ppermute x94, starting transfers between devices, flip(): lax.ppermute(value, axis, [(place, place ^ mask) for place in range(count)])  99.3 us
    all_to_all x12, waiting for transfers between devices, exchange(): lax.all_to_all(blocks, 'context', split_axis=0, concat_axis=0, tiled=True)  84.1 us
    dot_general x10, matrix products, dot_nt(): lax.dot_general(left_side, right_side, (((1,), (1,)), ((), ())), preferre...  71.2 us
    dot_general x14, matrix products, dot_nn(): return jnp.dot(left_side, right_side, preferred_element_type=F32)  69.3 us
    unnamed x362, local copies, waits for them, and re-layouts  66.4 us
    dot_general x16, matrix products, dot_tn(): lax.dot_general(left_side, right_side, (((0,), (0,)), ((), ())), preferre...  64 us
    all_to_all x12, starting transfers between devices, exchange(): lax.all_to_all(blocks, 'context', split_axis=0, concat_axis=0, tiled=True)  55.2 us
  transfers between devices with their start and end apart: 114, of which 46 were waited for; matrix products, arithmetic and copies ran while one was open for 46% of the time, Pallas kernels for 0%

profile of v2, /device:TPU:1, one launch (start us, length us, event | category | flops | bytes accessed | tf_op | source)
XLA Modules:
  0.0 974.6 jit_solution(3273620712999749942)
XLA Ops:
  7.0 10.4 %all-reduce.1 = s32[8,2]{1,0:T(8,128)S(1)} all-reduce(s32[8,2]{1,0:T(8,128)S(1)} %reshape.384), channel_id=2, replica_groups=mesh['section'=2,'context'=8,'tensor'=2] {'context'}, use_global_device_ids=true, to_apply=%add | all-reduce | flops 16 | bytes 128
  63.1 10.5 %collective-permute-done.10 = bf16[160,2048]{1,0:T(8,128)(2,1)S(1)} collective-permute-done((bf16[160,2048]{1,0:T(8,128)(2,1)}, bf16[160,2048]{1,0:T(8,128)(2,1)S(1)}, u32[]{:S(2)}, u32[]{:S(2)}) %collective-permute-start.10) | collective-permute-done | bytes 655392 | tf_op jit(solution)/shard_map/ppermute | solution.py:79
  78.8 4.8 all-to-all-start
  107.1 6.3 fusion.22
  163.1 10.6 %collective-permute-done.24 = bf16[80,2048]{1,0:T(8,128)(2,1)} collective-permute-done((bf16[80,2048]{1,0:T(8,128)(2,1)S(1)}, bf16[80,2048]{1,0:T(8,128)(2,1)}, u32[]{:S(2)}, u32[]{:S(2)}) %collective-permute-start.24) | collective-permute-done | bytes 327712 | tf_op jit(solution)/shard_map/ppermute | solution.py:79
  173.7 5.3 collective-permute-done.22
  213.6 9.8 %fusion.35 = (f32[1024,1024]{0,1:T(8,128)}, bf16[1024,1024]{0,1:T(8,128)(2,1)S(1)}) fusion(f32[1024]{0:T(1024)S(1)} %copy-done.142, bf16[1024,2048]{1,0:T(8,128)(2,1)S(1)} %copy-done.43, bf16[2048,512]{1,0:T(8,128)(2,1)S(1)} %collective-permute-done.25, bf16[2048,512]{1,0:T(8,128)(2,1)} %bitcast.29), kind=kOutput, calls=%fused_computation.58 | convolution fusion | flops 4314890240 | bytes 14684160 | tf_op jit(solution)/shard_map/dot_general | solution.py:70
  225.2 23.1 %collective-permute-done.28 = bf16[160,2048]{1,0:T(8,128)(2,1)} collective-permute-done((bf16[160,2048]{1,0:T(8,128)(2,1)S(1)}, bf16[160,2048]{1,0:T(8,128)(2,1)}, u32[]{:S(2)}, u32[]{:S(2)}) %collective-permute-start.28) | collective-permute-done | bytes 655392 | tf_op jit(solution)/shard_map/ppermute | solution.py:79
  261.1 5.2 convolution_convert_fusion.11
  274.0 5.6 convolution_convert_fusion.10
  281.8 15.3 %all-to-all-done.3 = bf16[8,256,384]{1,2,0:T(8,128)(2,1)S(1)} async-done(((bf16[8,256,384]{1,2,0:T(8,128)(2,1)}), bf16[8,256,384]{1,2,0:T(8,128)(2,1)S(1)}, u32[]{:S(2)}, u32[]{:S(2)}) %all-to-all-start.3) | async-done | bytes 1572896 | tf_op jit(solution)/shard_map/all_to_all | solution.py:275
  297.1 6.8 collective-permute-done.32
  310.7 5.7 collective-permute-done.35
  347.1 6.3 collective-permute-done.43
  367.6 5.5 collective-permute-start.45
  394.5 13.3 %all-to-all-done.4 = bf16[8,256,512]{2,1,0:T(8,128)(2,1)} async-done(((bf16[8,256,512]{2,1,0:T(8,128)(2,1)}), bf16[8,256,512]{2,1,0:T(8,128)(2,1)}, u32[]{:S(2)}, u32[]{:S(2)}) %all-to-all-start.4) | async-done | bytes 2097184 | tf_op jit(solution)/shard_map/all_to_all | solution.py:275
  407.8 7.5 all-to-all-start.5
  433.0 9.0 fusion.39
  448.3 4.9 collective-permute-done.48
  458.3 14.8 %all-to-all-done.5 = bf16[8,640,256]{1,2,0:T(8,128)(2,1)} async-done(((bf16[8,640,256]{1,2,0:T(8,128)(2,1)}), bf16[8,640,256]{1,2,0:T(8,128)(2,1)}, u32[]{:S(2)}, u32[]{:S(2)}) %all-to-all-start.5) | async-done | bytes 2621472 | tf_op jit(solution)/shard_map/all_to_all | solution.py:275
  488.2 9.0 fusion.225
  510.9 6.6 multiply_convert_fusion.1
  530.2 6.7 convolution_convert_fusion.4
  540.7 5.4 add_convert_fusion.5
  551.7 9.3 fusion.252
  561.0 10.4 %fusion.229 = (f32[2048]{0:T(1024)S(1)}, f32[2048]{0:T(1024)S(1)}, bf16[1024,2048]{1,0:T(8,128)(2,1)S(1)}, f32[2048]{0:T(1024)S(1)}, f32[2048]{0:T(1024)S(1)}) fusion(f32[1024]{0:T(1024)S(1)} %add_rsqrt_fusion, f32[1024]{0:T(1024)S(1)} %broadcast_multiply_fusion, bf16[1024,2048]{1,0:T(8,128)(2,1)S(1)} %copy-done.6, f32[2048]{0:T(1024)S(1)} %get-tuple-element.572, ...), kind=kOutput, calls=%fused_computation.553 | convolution fusion | flops 4330610688 | bytes 23126016 | tf_op jit(solution)/shard_map/dot_general | solution.py:64
  585.2 18.0 %collective-permute-done.54 = bf16[160,2048]{1,0:T(8,128)(2,1)} collective-permute-done((bf16[160,2048]{1,0:T(8,128)(2,1)}, bf16[160,2048]{1,0:T(8,128)(2,1)}, u32[]{:S(2)}, u32[]{:S(2)}) %collective-permute-start.54) | collective-permute-done | bytes 655392 | tf_op jit(solution)/shard_map/ppermute | solution.py:79
  612.1 7.3 collective-permute-done.57
  624.3 6.0 convolution_convert_fusion.9
  636.1 6.5 convolution_convert_fusion.8
  645.3 5.0 add_convert_fusion.7
  663.7 5.5 collective-permute-start.68
  681.5 5.7 add_convert_fusion.2
  688.9 21.0 %all-to-all-done.8 = bf16[8,256,384]{2,1,0:T(8,128)(2,1)S(1)} async-done(((bf16[8,256,384]{2,1,0:T(8,128)(2,1)}), bf16[8,256,384]{2,1,0:T(8,128)(2,1)S(1)}, u32[]{:S(2)}, u32[]{:S(2)}) %all-to-all-start.8) | async-done | bytes 1572896 | tf_op jit(solution)/shard_map/all_to_all | solution.py:275
  714.9 9.3 fusion.226
  738.8 8.6 multiply_convert_fusion
  761.6 5.3 add_convert_fusion.4
  766.9 6.8 all-to-all-done.9
  806.3 5.8 fusion.253
  812.1 11.8 %fusion.227 = (f32[2048]{0:T(1024)S(1)}, f32[2048]{0:T(1024)S(1)}, bf16[1024,2048]{1,0:T(8,128)(2,1)}, f32[2048]{0:T(1024)S(1)}, f32[2048]{0:T(1024)S(1)}) fusion(f32[1024]{0:T(1024)S(1)} %copy-done.137, f32[1024]{0:T(1024)S(1)} %copy-done.130, bf16[1024,2048]{1,0:T(8,128)(2,1)S(1)} %copy-done.10, f32[2048]{0:T(1024)S(1)} %copy-done.133, ...), kind=kOutput, calls=%fused_computation.551 | convolution fusion | flops 4330610688 | bytes 23126016 | tf_op jit(solution)/shard_map/dot_general | solution.py:64
  824.0 5.1 add_convert_fusion.6
  846.0 11.7 %collective-permute-done.78 = bf16[48,2048]{1,0:T(8,128)(2,1)S(1)} collective-permute-done((bf16[48,2048]{1,0:T(8,128)(2,1)S(1)}, bf16[48,2048]{1,0:T(8,128)(2,1)S(1)}, u32[]{:S(2)}, u32[]{:S(2)}) %collective-permute-start.78) | collective-permute-done | bytes 196640 | tf_op jit(solution)/shard_map/ppermute | solution.py:79
  866.2 9.6 collective-permute-done.86
  893.2 10.5 %collective-permute-done.95 = f32[2,24576]{1,0:T(2,128)S(1)} collective-permute-done((f32[2,24576]{1,0:T(2,128)S(1)}, f32[2,24576]{1,0:T(2,128)S(1)}, u32[]{:S(2)}, u32[]{:S(2)}) %collective-permute-start.95) | collective-permute-done | bytes 196640 | tf_op jit(solution)/shard_map/ppermute | solution.py:79
  905.2 6.2 collective-permute-start.96
  936.9 5.2 copy.189
  942.2 5.7 copy.192
  947.9 7.8 fusion.55
  (894 shorter events, 556.8 us)
Async XLA Ops:
  2.0 18.6 %collective-permute-start.1 = (bf16[128,2048]{1,0:T(8,128)(2,1)S(1)}, bf16[128,2048]{1,0:T(8,128)(2,1)S(1)}, u32[]{:S(2)}, u32[]{:S(2)}) collective-permute-start(bf16[128,2048]{1,0:T(8,128)(2,1)S(1)} %get-tuple-element.227), channel_id=1, source_target_pairs={{0,8},{2,10},{4,12},{6,14},{8,24},{10,26},{12,28},{14,30},{1,9},{3... | collective-permute-start | bytes 1572872 | tf_op jit(solution)/shard_map/ppermute | solution.py:256
  2.7 18.8 %collective-permute-start = (bf16[128,2048]{1,0:T(8,128)(2,1)S(1)}, bf16[128,2048]{1,0:T(8,128)(2,1)S(1)}, u32[]{:S(2)}, u32[]{:S(2)}) collective-permute-start(bf16[128,2048]{1,0:T(8,128)(2,1)S(1)} %get-tuple-element.226), channel_id=1, source_target_pairs={{0,0},{2,2},{4,4},{6,6},{8,16},{10,18},{12,20},{14,22},{1,1},{3,3}... | collective-permute-start | bytes 1572872 | tf_op jit(solution)/shard_map/ppermute | solution.py:256
  38.7 21.9 %collective-permute-start.12 = (bf16[128,2048]{1,0:T(8,128)(2,1)}, bf16[128,2048]{1,0:T(8,128)(2,1)S(1)}, u32[]{:S(2)}, u32[]{:S(2)}) collective-permute-start(bf16[128,2048]{1,0:T(8,128)(2,1)} %copy-done.118), channel_id=1, source_target_pairs={{16,0},{18,2},{20,4},{22,6},{24,16},{26,18},{28,20},{30,22},{17,1}... | collective-permute-start | bytes 1572872 | tf_op jit(solution)/shard_map/ppermute | solution.py:256
  42.0 20.9 %collective-permute-start.13 = (bf16[128,2048]{1,0:T(8,128)(2,1)}, bf16[128,2048]{1,0:T(8,128)(2,1)}, u32[]{:S(2)}, u32[]{:S(2)}) collective-permute-start(bf16[128,2048]{1,0:T(8,128)(2,1)} %copy-done.117), channel_id=1, source_target_pairs={{16,8},{18,10},{20,12},{22,14},{24,24},{26,26},{28,28},{30,30},{17... | collective-permute-start | bytes 1572872 | tf_op jit(solution)/shard_map/ppermute | solution.py:256
  56.0 18.9 %collective-permute-start.9 = (bf16[192,2048]{1,0:T(8,128)(2,1)S(1)}, bf16[192,2048]{1,0:T(8,128)(2,1)}, u32[]{:S(2)}, u32[]{:S(2)}) collective-permute-start(bf16[192,2048]{1,0:T(8,128)(2,1)S(1)} %pad_maximum_fusion.21), channel_id=1, source_target_pairs={{0,1},{1,0},{2,3},{3,2},{4,5},{5,4},{6,7},{7,6},{8,9},{9,8},{10,11... | collective-permute-start | bytes 2359304 | tf_op jit(solution)/shard_map/ppermute | solution.py:79
  78.8 39.1 %all-to-all-start = ((bf16[8,256,384]{1,2,0:T(8,128)(2,1)}), bf16[8,256,384]{1,2,0:T(8,128)(2,1)}, u32[]{:S(2)}, u32[]{:S(2)}) async-start(bf16[8,256,384]{1,2,0:T(8,128)(2,1)} %bitcast.14), calls=%async_computation | async-start | bytes 3145728 | tf_op jit(solution)/shard_map/all_to_all | solution.py:275
  84.9 30.8 %collective-permute-start.19 = (bf16[40,2048]{1,0:T(8,128)(2,1)S(1)}, bf16[40,2048]{1,0:T(8,128)(2,1)S(1)}, u32[]{:S(2)}, u32[]{:S(2)}) collective-permute-start(bf16[40,2048]{1,0:T(8,128)(2,1)S(1)} %get-tuple-element.552), channel_id=1, source_target_pairs={{0,1},{1,0},{2,3},{3,2},{4,5},{5,4},{6,7},{7,6},{8,9},{9,8},{10,11... | collective-permute-start | bytes 491528 | tf_op jit(solution)/shard_map/ppermute | solution.py:79
  85.0 30.7 %collective-permute-start.18 = (bf16[40,2048]{1,0:T(8,128)(2,1)S(1)}, bf16[40,2048]{1,0:T(8,128)(2,1)S(1)}, u32[]{:S(2)}, u32[]{:S(2)}) collective-permute-start(bf16[40,2048]{1,0:T(8,128)(2,1)S(1)} %get-tuple-element.553), channel_id=1, source_target_pairs={{0,4},{2,6},{4,0},{6,2},{8,12},{10,14},{12,8},{14,10},{1,5},{3,7},... | collective-permute-start | bytes 491528 | tf_op jit(solution)/shard_map/ppermute | solution.py:79
  93.7 19.7 %collective-permute-start.15 = (bf16[4,256,512]{2,1,0:T(8,128)(2,1)}, bf16[4,256,512]{2,1,0:T(8,128)(2,1)}, u32[]{:S(2)}, u32[]{:S(2)}) collective-permute-start(bf16[4,256,512]{2,1,0:T(8,128)(2,1)} %bitcast.221), channel_id=1, source_target_pairs={{0,16},{16,0},{1,17},{17,1},{2,18},{18,2},{3,19},{19,3},{4,20},{20... | collective-permute-start | bytes 3145736 | tf_op jit(solution)/shard_map/ppermute | solution.py:79
  130.5 53.0 %all-to-all-start.1 = ((bf16[8,256,512]{2,1,0:T(8,128)(2,1)}), bf16[8,256,512]{2,1,0:T(8,128)(2,1)}, u32[]{:S(2)}, u32[]{:S(2)}) async-start(bf16[8,256,512]{2,1,0:T(8,128)(2,1)} %bitcast.20), calls=%async_computation.1 | async-start | bytes 4194304 | tf_op jit(solution)/shard_map/all_to_all | solution.py:275
  154.7 18.9 %collective-permute-start.24 = (bf16[80,2048]{1,0:T(8,128)(2,1)S(1)}, bf16[80,2048]{1,0:T(8,128)(2,1)}, u32[]{:S(2)}, u32[]{:S(2)}) collective-permute-start(bf16[80,2048]{1,0:T(8,128)(2,1)S(1)} %pad_maximum_fusion.48), channel_id=1, source_target_pairs={{0,2},{2,0},{4,6},{6,4},{8,10},{10,8},{12,14},{14,12},{1,3},{3,1},... | collective-permute-start | bytes 983048 | tf_op jit(solution)/shard_map/ppermute | solution.py:79
  156.6 22.3 %collective-permute-start.22 = (bf16[96,2048]{1,0:T(8,128)(2,1)S(1)}, bf16[96,2048]{1,0:T(8,128)(2,1)}, u32[]{:S(2)}, u32[]{:S(2)}) collective-permute-start(bf16[96,2048]{1,0:T(8,128)(2,1)S(1)} %pad_maximum_fusion.39), channel_id=1, source_target_pairs={{0,4},{2,6},{4,0},{6,2},{8,12},{10,14},{12,8},{14,10},{1,5},{3,7},... | collective-permute-start | bytes 1179656 | tf_op jit(solution)/shard_map/ppermute | solution.py:79
  186.5 63.5 %all-to-all-start.2 = ((bf16[8,640,256]{1,2,0:T(8,128)(2,1)}), bf16[8,640,256]{1,2,0:T(8,128)(2,1)}, u32[]{:S(2)}, u32[]{:S(2)}) async-start(bf16[8,640,256]{1,2,0:T(8,128)(2,1)} %bitcast.195), calls=%async_computation.2 | async-start | bytes 5242880 | tf_op jit(solution)/shard_map/all_to_all | solution.py:275
  193.5 54.8 %collective-permute-start.28 = (bf16[160,2048]{1,0:T(8,128)(2,1)S(1)}, bf16[160,2048]{1,0:T(8,128)(2,1)}, u32[]{:S(2)}, u32[]{:S(2)}) collective-permute-start(bf16[160,2048]{1,0:T(8,128)(2,1)S(1)} %pad_maximum_fusion.28), channel_id=1, source_target_pairs={{0,4},{2,6},{4,0},{6,2},{8,12},{10,14},{12,8},{14,10},{1,5},{3,7},... | collective-permute-start | bytes 1966088 | tf_op jit(solution)/shard_map/ppermute | solution.py:79
  195.0 53.3 %collective-permute-start.27 = (bf16[160,2048]{1,0:T(8,128)(2,1)S(1)}, bf16[160,2048]{1,0:T(8,128)(2,1)}, u32[]{:S(2)}, u32[]{:S(2)}) collective-permute-start(bf16[160,2048]{1,0:T(8,128)(2,1)S(1)} %pad_maximum_fusion.27), channel_id=1, source_target_pairs={{0,2},{2,0},{4,6},{6,4},{8,10},{10,8},{12,14},{14,12},{1,3},{3,1},... | collective-permute-start | bytes 1966088 | tf_op jit(solution)/shard_map/ppermute | solution.py:79
  197.2 51.1 %collective-permute-start.26 = (bf16[192,2048]{1,0:T(8,128)(2,1)S(1)}, bf16[192,2048]{1,0:T(8,128)(2,1)}, u32[]{:S(2)}, u32[]{:S(2)}) collective-permute-start(bf16[192,2048]{1,0:T(8,128)(2,1)S(1)} %pad_maximum_fusion.22), channel_id=1, source_target_pairs={{0,1},{1,0},{2,3},{3,2},{4,5},{5,4},{6,7},{7,6},{8,9},{9,8},{10,11... | collective-permute-start | bytes 2359304 | tf_op jit(solution)/shard_map/ppermute | solution.py:79
  256.2 40.8 %all-to-all-start.3 = ((bf16[8,256,384]{1,2,0:T(8,128)(2,1)}), bf16[8,256,384]{1,2,0:T(8,128)(2,1)S(1)}, u32[]{:S(2)}, u32[]{:S(2)}) async-start(bf16[8,256,384]{1,2,0:T(8,128)(2,1)} %bitcast.30), calls=%async_computation.3 | async-start | bytes 3145728 | tf_op jit(solution)/shard_map/all_to_all | solution.py:275
  267.7 29.4 %collective-permute-start.31 = (bf16[160,2048]{1,0:T(8,128)(2,1)}, bf16[160,2048]{1,0:T(8,128)(2,1)}, u32[]{:S(2)}, u32[]{:S(2)}) collective-permute-start(bf16[160,2048]{1,0:T(8,128)(2,1)} %slice.891), channel_id=1, source_target_pairs={{0,2},{2,0},{4,6},{6,4},{8,10},{10,8},{12,14},{14,12},{1,3},{3,1},... | collective-permute-start | bytes 1966088 | tf_op jit(solution)/shard_map/ppermute | solution.py:79
  273.9 30.0 %collective-permute-start.30 = (bf16[192,2048]{1,0:T(8,128)(2,1)S(1)}, bf16[192,2048]{1,0:T(8,128)(2,1)S(1)}, u32[]{:S(2)}, u32[]{:S(2)}) collective-permute-start(bf16[192,2048]{1,0:T(8,128)(2,1)S(1)} %slice.890), channel_id=1, source_target_pairs={{0,1},{1,0},{2,3},{3,2},{4,5},{5,4},{6,7},{7,6},{8,9},{9,8},{10,11... | collective-permute-start | bytes 2359304 | tf_op jit(solution)/shard_map/ppermute | solution.py:79
  280.6 23.3 %collective-permute-start.32 = (bf16[160,2048]{1,0:T(8,128)(2,1)}, bf16[160,2048]{1,0:T(8,128)(2,1)}, u32[]{:S(2)}, u32[]{:S(2)}) collective-permute-start(bf16[160,2048]{1,0:T(8,128)(2,1)} %slice.892), channel_id=1, source_target_pairs={{0,4},{2,6},{4,0},{6,2},{8,12},{10,14},{12,8},{14,10},{1,5},{3,7},... | collective-permute-start | bytes 1966088 | tf_op jit(solution)/shard_map/ppermute | solution.py:79
  358.4 49.4 %all-to-all-start.4 = ((bf16[8,256,512]{2,1,0:T(8,128)(2,1)}), bf16[8,256,512]{2,1,0:T(8,128)(2,1)}, u32[]{:S(2)}, u32[]{:S(2)}) async-start(bf16[8,256,512]{2,1,0:T(8,128)(2,1)} %bitcast.32), calls=%async_computation.4 | async-start | bytes 4194304 | tf_op jit(solution)/shard_map/all_to_all | solution.py:275
  407.8 65.4 %all-to-all-start.5 = ((bf16[8,640,256]{1,2,0:T(8,128)(2,1)}), bf16[8,640,256]{1,2,0:T(8,128)(2,1)}, u32[]{:S(2)}, u32[]{:S(2)}) async-start(bf16[8,640,256]{1,2,0:T(8,128)(2,1)} %bitcast.192), calls=%async_computation.5 | async-start | bytes 5242880 | tf_op jit(solution)/shard_map/all_to_all | solution.py:275
  483.8 64.0 %all-to-all-start.6 = ((bf16[8,640,256]{2,1,0:T(8,128)(2,1)}), bf16[8,640,256]{2,1,0:T(8,128)(2,1)}, u32[]{:S(2)}, u32[]{:S(2)}) async-start(bf16[8,640,256]{2,1,0:T(8,128)(2,1)} %bitcast.193), calls=%async_computation.6 | async-start | bytes 5242880 | tf_op jit(solution)/shard_map/all_to_all | solution.py:275
  506.1 34.6 %collective-permute-start.50 = (bf16[2048,512]{1,0:T(8,128)(2,1)}, bf16[2048,512]{1,0:T(8,128)(2,1)}, u32[]{:S(2)}, u32[]{:S(2)}) collective-permute-start(bf16[2048,512]{1,0:T(8,128)(2,1)} %convolution_convert_fusion.3), channel_id=1, source_target_pairs={{0,16},{16,0},{1,17},{17,1},{2,18},{18,2},{3,19},{19,3},{4,20},{20... | collective-permute-start | bytes 6291464 | tf_op jit(solution)/shard_map/ppermute | solution.py:79
  547.8 55.5 %all-to-all-start.7 = ((bf16[8,256,512]{2,1,0:T(8,128)(2,1)}), bf16[8,256,512]{2,1,0:T(8,128)(2,1)S(1)}, u32[]{:S(2)}, u32[]{:S(2)}) async-start(bf16[8,256,512]{2,1,0:T(8,128)(2,1)} %bitcast.217), calls=%async_computation.7 | async-start | bytes 4194304 | tf_op jit(solution)/shard_map/all_to_all | solution.py:275
  571.4 31.8 %collective-permute-start.52 = (bf16[192,2048]{1,0:T(8,128)(2,1)S(1)}, bf16[192,2048]{1,0:T(8,128)(2,1)}, u32[]{:S(2)}, u32[]{:S(2)}) collective-permute-start(bf16[192,2048]{1,0:T(8,128)(2,1)S(1)} %slice.930), channel_id=1, source_target_pairs={{0,1},{1,0},{2,3},{3,2},{4,5},{5,4},{6,7},{7,6},{8,9},{9,8},{10,11... | collective-permute-start | bytes 2359304 | tf_op jit(solution)/shard_map/ppermute | solution.py:79
  573.2 30.1 %collective-permute-start.54 = (bf16[160,2048]{1,0:T(8,128)(2,1)}, bf16[160,2048]{1,0:T(8,128)(2,1)}, u32[]{:S(2)}, u32[]{:S(2)}) collective-permute-start(bf16[160,2048]{1,0:T(8,128)(2,1)} %get-tuple-element.508), channel_id=1, source_target_pairs={{0,4},{2,6},{4,0},{6,2},{8,12},{10,14},{12,8},{14,10},{1,5},{3,7},... | collective-permute-start | bytes 1966088 | tf_op jit(solution)/shard_map/ppermute | solution.py:79
  574.6 28.6 %collective-permute-start.53 = (bf16[160,2048]{1,0:T(8,128)(2,1)}, bf16[160,2048]{1,0:T(8,128)(2,1)}, u32[]{:S(2)}, u32[]{:S(2)}) collective-permute-start(bf16[160,2048]{1,0:T(8,128)(2,1)} %get-tuple-element.509), channel_id=1, source_target_pairs={{0,2},{2,0},{4,6},{6,4},{8,10},{10,8},{12,14},{14,12},{1,3},{3,1},... | collective-permute-start | bytes 1966088 | tf_op jit(solution)/shard_map/ppermute | solution.py:79
  583.5 61.9 %collective-permute-start.67 = (bf16[2048,384]{1,0:T(8,128)(2,1)}, bf16[2048,384]{1,0:T(8,128)(2,1)}, u32[]{:S(2)}, u32[]{:S(2)}) collective-permute-start(bf16[2048,384]{1,0:T(8,128)(2,1)} %convolution_convert_fusion.7), channel_id=1, source_target_pairs={{0,16},{16,0},{1,17},{17,1},{2,18},{18,2},{3,19},{19,3},{4,20},{20... | collective-permute-start | bytes 4718600 | tf_op jit(solution)/shard_map/ppermute | solution.py:79
  663.7 17.8 %collective-permute-start.68 = (bf16[640,2048]{1,0:T(8,128)(2,1)}, bf16[640,2048]{1,0:T(8,128)(2,1)}, u32[]{:S(2)}, u32[]{:S(2)}) collective-permute-start(bf16[640,2048]{1,0:T(8,128)(2,1)} %convolution_convert_fusion), channel_id=1, source_target_pairs={{0,16},{16,0},{1,17},{17,1},{2,18},{18,2},{3,19},{19,3},{4,20},{20... | collective-permute-start | bytes 7864328 | tf_op jit(solution)/shard_map/ppermute | solution.py:79
  669.3 40.5 %all-to-all-start.8 = ((bf16[8,256,384]{2,1,0:T(8,128)(2,1)}), bf16[8,256,384]{2,1,0:T(8,128)(2,1)S(1)}, u32[]{:S(2)}, u32[]{:S(2)}) async-start(bf16[8,256,384]{2,1,0:T(8,128)(2,1)} %bitcast.219), calls=%async_computation.8 | async-start | bytes 3145728 | tf_op jit(solution)/shard_map/all_to_all | solution.py:275
  675.3 91.6 %collective-permute-start.70 = (bf16[192,2048]{1,0:T(8,128)(2,1)}, bf16[192,2048]{1,0:T(8,128)(2,1)}, u32[]{:S(2)}, u32[]{:S(2)}) collective-permute-start(bf16[192,2048]{1,0:T(8,128)(2,1)} %slice.801), channel_id=1, source_target_pairs={{0,1},{1,0},{2,3},{3,2},{4,5},{5,4},{6,7},{7,6},{8,9},{9,8},{10,11... | collective-permute-start | bytes 2359304 | tf_op jit(solution)/shard_map/ppermute | solution.py:79
  678.0 88.9 %collective-permute-start.71 = (bf16[160,2048]{1,0:T(8,128)(2,1)}, bf16[160,2048]{1,0:T(8,128)(2,1)}, u32[]{:S(2)}, u32[]{:S(2)}) collective-permute-start(bf16[160,2048]{1,0:T(8,128)(2,1)} %slice.802), channel_id=1, source_target_pairs={{0,2},{2,0},{4,6},{6,4},{8,10},{10,8},{12,14},{14,12},{1,3},{3,1},... | collective-permute-start | bytes 1966088 | tf_op jit(solution)/shard_map/ppermute | solution.py:79
  680.3 86.6 %collective-permute-start.72 = (bf16[160,2048]{1,0:T(8,128)(2,1)}, bf16[160,2048]{1,0:T(8,128)(2,1)}, u32[]{:S(2)}, u32[]{:S(2)}) collective-permute-start(bf16[160,2048]{1,0:T(8,128)(2,1)} %slice.803), channel_id=1, source_target_pairs={{0,4},{2,6},{4,0},{6,2},{8,12},{10,14},{12,8},{14,10},{1,5},{3,7},... | collective-permute-start | bytes 1966088 | tf_op jit(solution)/shard_map/ppermute | solution.py:79
  711.0 62.7 %all-to-all-start.9 = ((bf16[8,640,256]{2,1,0:T(8,128)(2,1)}), bf16[8,640,256]{2,1,0:T(8,128)(2,1)S(1)}, u32[]{:S(2)}, u32[]{:S(2)}) async-start(bf16[8,640,256]{2,1,0:T(8,128)(2,1)} %bitcast.194), calls=%async_computation.9 | async-start | bytes 5242880 | tf_op jit(solution)/shard_map/all_to_all | solution.py:275
  733.2 26.4 %collective-permute-start.69 = (bf16[2048,512]{1,0:T(8,128)(2,1)}, bf16[2048,512]{1,0:T(8,128)(2,1)}, u32[]{:S(2)}, u32[]{:S(2)}) collective-permute-start(bf16[2048,512]{1,0:T(8,128)(2,1)} %convolution_convert_fusion.2), channel_id=1, source_target_pairs={{0,16},{16,0},{1,17},{17,1},{2,18},{18,2},{3,19},{19,3},{4,20},{20... | collective-permute-start | bytes 6291464 | tf_op jit(solution)/shard_map/ppermute | solution.py:79
  780.3 53.0 %all-to-all-start.10 = ((bf16[8,256,512]{2,1,0:T(8,128)(2,1)}), bf16[8,256,512]{2,1,0:T(8,128)(2,1)}, u32[]{:S(2)}, u32[]{:S(2)}) async-start(bf16[8,256,512]{2,1,0:T(8,128)(2,1)} %bitcast.216), calls=%async_computation.10 | async-start | bytes 4194304 | tf_op jit(solution)/shard_map/all_to_all | solution.py:275
  794.7 35.7 %collective-permute-start.75 = (bf16[96,2048]{1,0:T(8,128)(2,1)S(1)}, bf16[96,2048]{1,0:T(8,128)(2,1)}, u32[]{:S(2)}, u32[]{:S(2)}) collective-permute-start(bf16[96,2048]{1,0:T(8,128)(2,1)S(1)} %slice.951), channel_id=1, source_target_pairs={{0,4},{2,6},{4,0},{6,2},{8,12},{10,14},{12,8},{14,10},{1,5},{3,7},... | collective-permute-start | bytes 1179656 | tf_op jit(solution)/shard_map/ppermute | solution.py:79
  797.5 31.5 %collective-permute-start.76 = (bf16[80,2048]{1,0:T(8,128)(2,1)S(1)}, bf16[80,2048]{1,0:T(8,128)(2,1)S(1)}, u32[]{:S(2)}, u32[]{:S(2)}) collective-permute-start(bf16[80,2048]{1,0:T(8,128)(2,1)S(1)} %slice.952), channel_id=1, source_target_pairs={{0,1},{1,0},{2,3},{3,2},{4,5},{5,4},{6,7},{7,6},{8,9},{9,8},{10,11... | collective-permute-start | bytes 983048 | tf_op jit(solution)/shard_map/ppermute | solution.py:79
  800.0 29.0 %collective-permute-start.77 = (bf16[80,2048]{1,0:T(8,128)(2,1)S(1)}, bf16[80,2048]{1,0:T(8,128)(2,1)S(1)}, u32[]{:S(2)}, u32[]{:S(2)}) collective-permute-start(bf16[80,2048]{1,0:T(8,128)(2,1)S(1)} %slice.953), channel_id=1, source_target_pairs={{0,2},{2,0},{4,6},{6,4},{8,10},{10,8},{12,14},{14,12},{1,3},{3,1},... | collective-permute-start | bytes 983048 | tf_op jit(solution)/shard_map/ppermute | solution.py:79
  805.1 18.9 %collective-permute-start.74 = (bf16[2048,384]{1,0:T(8,128)(2,1)}, bf16[2048,384]{1,0:T(8,128)(2,1)}, u32[]{:S(2)}, u32[]{:S(2)}) collective-permute-start(bf16[2048,384]{1,0:T(8,128)(2,1)} %convolution_convert_fusion.6), channel_id=1, source_target_pairs={{0,16},{16,0},{1,17},{17,1},{2,18},{18,2},{3,19},{19,3},{4,20},{20... | collective-permute-start | bytes 4718600 | tf_op jit(solution)/shard_map/ppermute | solution.py:79
  836.8 21.2 %collective-permute-start.82 = (bf16[192,2048]{1,0:T(8,128)(2,1)S(1)}, bf16[192,2048]{1,0:T(8,128)(2,1)S(1)}, u32[]{:S(2)}, u32[]{:S(2)}) collective-permute-start(bf16[192,2048]{1,0:T(8,128)(2,1)S(1)} %slice.832), channel_id=1, source_target_pairs={{0,1},{1,0},{2,3},{3,2},{4,5},{5,4},{6,7},{7,6},{8,9},{9,8},{10,11... | collective-permute-start | bytes 2359304 | tf_op jit(solution)/shard_map/ppermute | solution.py:79
  837.8 20.0 %collective-permute-start.84 = (bf16[160,2048]{1,0:T(8,128)(2,1)S(1)}, bf16[160,2048]{1,0:T(8,128)(2,1)S(1)}, u32[]{:S(2)}, u32[]{:S(2)}) collective-permute-start(bf16[160,2048]{1,0:T(8,128)(2,1)S(1)} %get-tuple-element.503), channel_id=1, source_target_pairs={{0,4},{2,6},{4,0},{6,2},{8,12},{10,14},{12,8},{14,10},{1,5},{3,7},... | collective-permute-start | bytes 1966088 | tf_op jit(solution)/shard_map/ppermute | solution.py:79
  839.2 18.5 %collective-permute-start.83 = (bf16[160,2048]{1,0:T(8,128)(2,1)S(1)}, bf16[160,2048]{1,0:T(8,128)(2,1)S(1)}, u32[]{:S(2)}, u32[]{:S(2)}) collective-permute-start(bf16[160,2048]{1,0:T(8,128)(2,1)S(1)} %get-tuple-element.504), channel_id=1, source_target_pairs={{0,2},{2,0},{4,6},{6,4},{8,10},{10,8},{12,14},{14,12},{1,3},{3,1},... | collective-permute-start | bytes 1966088 | tf_op jit(solution)/shard_map/ppermute | solution.py:79
  903.7 59.8 %collective-permute-start.97 = (bf16[128,2048]{1,0:T(8,128)(2,1)}, bf16[128,2048]{1,0:T(8,128)(2,1)}, u32[]{:S(2)}, u32[]{:S(2)}) collective-permute-start(bf16[128,2048]{1,0:T(8,128)(2,1)} %fusion.84), channel_id=1, source_target_pairs={{8,0},{10,2},{12,4},{14,6},{24,8},{26,10},{28,12},{30,14},{9,1},{1... | collective-permute-start | bytes 1572872 | tf_op jit(solution)/shard_map/ppermute | solution.py:267
  905.2 58.3 %collective-permute-start.96 = (bf16[128,2048]{1,0:T(8,128)(2,1)}, bf16[128,2048]{1,0:T(8,128)(2,1)}, u32[]{:S(2)}, u32[]{:S(2)}) collective-permute-start(bf16[128,2048]{1,0:T(8,128)(2,1)} %fusion.84), channel_id=1, source_target_pairs={{0,0},{2,2},{4,4},{6,6},{16,8},{18,10},{20,12},{22,14},{1,1},{3,3}... | collective-permute-start | bytes 1572872 | tf_op jit(solution)/shard_map/ppermute | solution.py:267
  912.0 43.7 %all-to-all-start.11 = ((bf16[8,256,384]{2,1,0:T(8,128)(2,1)}), bf16[8,256,384]{2,1,0:T(8,128)(2,1)}, u32[]{:S(2)}, u32[]{:S(2)}) async-start(bf16[8,256,384]{2,1,0:T(8,128)(2,1)} %bitcast.218), calls=%async_computation.11 | async-start | bytes 3145728 | tf_op jit(solution)/shard_map/all_to_all | solution.py:275
  928.6 19.4 %collective-permute-start.99 = (bf16[4,640,256]{2,0,1:T(4,128)(2,1)}, bf16[4,640,256]{2,0,1:T(4,128)(2,1)}, u32[]{:S(2)}, u32[]{:S(2)}) collective-permute-start(bf16[4,640,256]{2,0,1:T(4,128)(2,1)} %select_convert_fusion), channel_id=1, source_target_pairs={{0,16},{16,0},{1,17},{17,1},{2,18},{18,2},{3,19},{19,3},{4,20},{20... | collective-permute-start | bytes 3932168 | tf_op jit(solution)/shard_map/ppermute | solution.py:79
  (221 other events, 2107.6 us)
